TPU v7x, 32 devices: a whole 2x2x4 slice. The times are simulated.
32 devices in a mesh: dom: 4 (over x, core), band: 8 (over z, y).
Axes of the slice: x: 2, y: 2, z: 4, core: 2. Of those that a mesh axis runs over, the one named last changes fastest.
Arguments:
- wavefunctions: bfloat16 [128, 32, 128, 128], P('band', 'dom'), may hold values from -6 to 6
- potential: float32 [32, 128, 128], P('dom'), may hold values from -3 to 1
- projectors: bfloat16 [144, 8, 1024], P('dom'), may hold values from -0.1875 to 0.1875
- margin_atoms: int32 [144], P('dom'), may hold values from 0 to 47, as said below
- tile_rows: int32 [144], P('dom'), may hold values from 0 to 1016
- coupling: float32 [8, 8], replicated, may hold values from -4 to 4
- band_weights: float32 [128], P('band'), may hold values from 0.005 to 0.03
Outputs:
- applied: bfloat16 [128, 32, 128, 128], P('band', 'dom')
- forces: float32 [3, 48], P(None, 'dom')
Inputs may be any that keep to these rules, and one draw needn't show every extreme that they name: `margin_atoms`: the list of domain d holds each atom a with a // 12 equal to d - 1, d or d + 1 (cyclically over the domains) exactly once, in an order drawn from the seed; so every atom is listed in three domains.
All inputs are finite; a program needn't handle non-finite values.
Results may differ from a plain program's by a relative error of at most 0.0095.
Values may be sent and summed in bfloat16 or wider, within the bound.
A program may use at most 128 MiB of HBM per device.

v0:
```python
import functools

import jax
import jax.numpy as jnp
import numpy as np
from jax import lax
from jax.experimental import pallas as pl
from jax.experimental.pallas import tpu as pltpu
from jax.sharding import PartitionSpec as P

ATOM_DEV = 12
LANES = 128
ROWS = 16
VMEM_LIMIT = 52 * 1024 * 1024
F32 = jnp.float32
BF16 = jnp.bfloat16
HIGHEST = lax.Precision.HIGHEST


def vmem():
    return pl.BlockSpec(memory_space=pltpu.VMEM)


def smem():
    return pl.BlockSpec(memory_space=pltpu.SMEM)


def dot(a, b):
    return jnp.dot(a, b, preferred_element_type=F32)


def dot_nt(a, b, precision=None):
    return lax.dot_general(
        a, b, (((1,), (1,)), ((), ())), precision=precision, preferred_element_type=F32
    )


def circulant(width, taps):
    table = np.zeros((width, width), np.float32)
    for offset, value in taps.items():
        for target in range(width):
            table[(target + offset) % width, target] += value
    return table


def band_swap(band_count, band_pad):
    table = np.zeros((ROWS * band_pad, band_count * ROWS), np.float32)
    for y in range(ROWS):
        for b in range(band_count):
            table[y * band_pad + b, b * ROWS + y] = 1.0
    return table


def measure_tiles(field_ref, proj_ref, rows_ref, lhs_ref, meas_ref, entry_count, proj_count, depth):
    height = field_ref.shape[1]
    group = LANES // proj_count
    meas_ref[...] = jnp.zeros_like(meas_ref)
    for start in range(0, entry_count, group):
        count = min(group, entry_count - start)
        for k in range(count):
            row = rows_ref[start + k]
            tile = field_ref[pl.ds(row, depth)]
            for j in range(depth):
                lhs_ref[k * height : (k + 1) * height, j * LANES : (j + 1) * LANES] = tile[j]
        width = count * proj_count
        whole = dot_nt(
            lhs_ref[: count * height],
            proj_ref[start * proj_count : start * proj_count + width],
        )
        whole = whole.reshape(count, height, width)
        lane = lax.broadcasted_iota(jnp.int32, (count, height, width), 2) // proj_count
        item = lax.broadcasted_iota(jnp.int32, (count, height, width), 0)
        picked = jnp.sum(jnp.where(lane == item, whole, 0.0), axis=0)
        meas_ref[:, start * proj_count : start * proj_count + width] = picked


def margin_kernel(
    dims, wave_ref, proj_ref, rows_ref, swap_ref, sort_ref, turned_ref, table_ref, lhs_ref, meas_ref
):
    band_count, band_pad, plane_count, width_y, entry_count, proj_count, depth = dims

    def turn(step, carry):
        for x in range(plane_count):
            block = wave_ref[:, x, pl.ds(pl.multiple_of(step * ROWS, ROWS), ROWS), :]
            moved = dot(swap_ref[...], block.reshape(band_count * ROWS, LANES)).astype(BF16)
            turned_ref[pl.ds(x * width_y + step * ROWS, ROWS)] = moved.reshape(
                ROWS, band_pad, LANES
            )
        return carry

    lax.fori_loop(0, width_y // ROWS, turn, 0)
    measure_tiles(
        turned_ref, proj_ref, rows_ref, lhs_ref, meas_ref, entry_count, proj_count, depth
    )
    table_ref[...] = dot(meas_ref[...].astype(BF16), sort_ref[...]).astype(BF16)


def gradient_kernel(
    dims, turned_ref, proj_ref, rows_ref, first_ref, meas_ref, field_ref, lhs_ref
):
    band_count, band_pad, plane_count, width_y, entry_count, proj_count, depth = dims

    def rows_of(x, y, count):
        return turned_ref[pl.ds(x * width_y + y, count)].astype(F32)

    def step_rows(step, carry):
        y = step * ROWS
        before = lax.rem(y + width_y - 2, width_y)
        after = lax.rem(y + ROWS, width_y)
        for x in range(plane_count):
            here = turned_ref[pl.ds(x * width_y + y, ROWS)]
            wide = jnp.concatenate(
                [rows_of(x, before, 2), here.astype(F32), rows_of(x, after, 2)], axis=0
            )
            along_y = wide[:ROWS] - wide[4:] + 8.0 * (wide[3 : ROWS + 3] - wide[1 : ROWS + 1])
            along_x = jnp.zeros((ROWS, band_pad, LANES), F32)
            for offset, value in ((-2, 1.0), (-1, -8.0), (1, 8.0), (2, -1.0)):
                if 0 <= x + offset < plane_count:
                    along_x = along_x + value * rows_of(x + offset, y, ROWS)
            along_z = dot(here.reshape(ROWS * band_pad, LANES), first_ref[...]).reshape(
                ROWS, band_pad, LANES
            )
            rows = pl.ds(x * width_y + y, ROWS)
            field_ref[rows, :band_pad] = (along_x * (1.0 / 12.0)).astype(BF16)
            field_ref[rows, band_pad : 2 * band_pad] = (along_y * (1.0 / 12.0)).astype(BF16)
            field_ref[rows, 2 * band_pad :] = (along_z * (1.0 / 12.0)).astype(BF16)
        return carry

    lax.fori_loop(0, width_y // ROWS, step_rows, 0)
    measure_tiles(field_ref, proj_ref, rows_ref, lhs_ref, meas_ref, entry_count, proj_count, depth)


def apply_kernel(
    dims, places, *refs
):
    band_count, band_pad, plane_count, width_y, entry_count, proj_count, depth = dims
    table_refs = refs[: len(places)]
    (
        wave_ref, pot_ref, proj_ref, rows_ref, swap_ref, sort_ref, mix_ref, second_y_ref,
        second_z_ref, out_ref, edge_ref, coef_ref, acc_ref, part_ref,
    ) = refs[len(places) :]
    shifts = dict(places)
    scaled = []
    for s in (-1, 0, 1):
        total = jnp.zeros((band_pad, LANES), F32)
        for u in (s - 1, s, s + 1):
            block = s - u + 1
            held = table_refs[shifts[u]][:, block * LANES : (block + 1) * LANES]
            total = total + held.astype(F32)
        scaled.append(jnp.dot(total, mix_ref[...], precision=HIGHEST, preferred_element_type=F32))
    scaled = jnp.concatenate(scaled, axis=1)
    coef = dot_nt(scaled, sort_ref[...].astype(F32), HIGHEST)
    coef_ref[...] = coef
    half = coef.astype(BF16)

    acc_ref[...] = jnp.zeros_like(acc_ref)
    group = LANES // proj_count
    for start in range(0, entry_count, group):
        count = min(group, entry_count - start)
        width = count * proj_count
        first = start * proj_count
        held = jnp.broadcast_to(
            half[:, first : first + width].astype(F32)[None], (count, band_pad, width)
        )
        lane = lax.broadcasted_iota(jnp.int32, (count, band_pad, width), 2) // proj_count
        item = lax.broadcasted_iota(jnp.int32, (count, band_pad, width), 0)
        spread = jnp.where(lane == item, held, 0.0).reshape(count * band_pad, width).astype(BF16)
        for j in range(depth):
            terms = dot(
                spread, proj_ref[first : first + width, j * LANES : (j + 1) * LANES]
            )
            for k in range(count):
                row = rows_ref[start + k] + j
                acc_ref[row] += terms[k * band_pad : (k + 1) * band_pad]

    def turn_back(step, carry):
        for x in range(plane_count):
            block = acc_ref[pl.ds(x * width_y + step * ROWS, ROWS)].astype(BF16)
            moved = lax.dot_general(
                swap_ref[...],
                block.reshape(ROWS * band_pad, LANES),
                (((0,), (0,)), ((), ())),
                preferred_element_type=F32,
            ).astype(BF16)
            part_ref[:, x, pl.ds(pl.multiple_of(step * ROWS, ROWS), ROWS), :] = moved.reshape(
                band_count, ROWS, LANES
            )
        return carry

    lax.fori_loop(0, width_y // ROWS, turn_back, 0)

    def each_band(b, carry):
        for x in range(plane_count):
            here = wave_ref[b, x]
            lap = dot(second_y_ref[...], here) + dot(here, second_z_ref[...])
            for offset, value in ((-2, -1.0), (-1, 16.0), (1, 16.0), (2, -1.0)):
                if 0 <= x + offset < plane_count:
                    lap = lap + value * wave_ref[b, x + offset].astype(F32)
            total = lap * (-1.0 / 24.0) + pot_ref[x] * here.astype(F32)
            total = total + part_ref[b, x].astype(F32)
            if x < 2:
                edge_ref[b, x] = total
            elif x >= plane_count - 2:
                edge_ref[b, x - plane_count + 4] = total
            else:
                out_ref[b, x] = total.astype(BF16)
        return carry

    lax.fori_loop(0, band_count, each_band, 0)


def force_kernel(
    dims, before_ref, after_ref, proj_ref, rows_ref, swap_ref, meas_ref, coef_ref, weight_ref,
    pick_ref, out_ref, field_ref, lhs_ref, extra_ref,
):
    band_count, band_pad, plane_count, width_y, entry_count, proj_count, depth = dims
    inner = (plane_count - 4) * width_y
    field_ref[2 * width_y : 2 * width_y + inner] = jnp.zeros((inner, band_pad, LANES), BF16)

    def step_rows(step, carry):
        rows = pl.ds(pl.multiple_of(step * ROWS, ROWS), ROWS)
        b2 = before_ref[:, 0, rows, :].astype(F32)
        b1 = before_ref[:, 1, rows, :].astype(F32)
        a1 = after_ref[:, 0, rows, :].astype(F32)
        a2 = after_ref[:, 1, rows, :].astype(F32)
        last = plane_count - 1
        for x, value in ((0, b2 - 8.0 * b1), (1, b1), (last - 1, -a1), (last, 8.0 * a1 - a2)):
            value = (value * (1.0 / 12.0)).astype(BF16)
            moved = dot(swap_ref[...], value.reshape(band_count * ROWS, LANES)).astype(BF16)
            field_ref[pl.ds(x * width_y + step * ROWS, ROWS)] = moved.reshape(
                ROWS, band_pad, LANES
            )
        return carry

    lax.fori_loop(0, width_y // ROWS, step_rows, 0)
    measure_tiles(
        field_ref, proj_ref, rows_ref, lhs_ref, extra_ref, entry_count, proj_count, depth
    )
    weighted = coef_ref[...] * weight_ref[...]
    sums = []
    for k in range(3):
        held = meas_ref[k * band_pad : (k + 1) * band_pad]
        if k == 0:
            held = held + extra_ref[...]
        sums.append(jnp.sum(weighted * held, axis=0, keepdims=True))
    sums = jnp.concatenate(sums + [jnp.zeros((5, sums[0].shape[1]), F32)], axis=0)
    for s in range(3):
        out_ref[s] = jnp.dot(
            sums,
            pick_ref[:, s * LANES : (s + 1) * LANES].astype(F32),
            precision=HIGHEST,
            preferred_element_type=F32,
        )


def reduce_kernel(dom_count, band_devices, part_ref, out_ref, held_ref, send_sem, recv_sem):
    own = lax.axis_index("dom")
    band = lax.axis_index("band")
    partners = [
        (s, t) for t in range(band_devices) for s in (-1, 0, 1) if (s, t) != (0, 0)
    ]

    def device(s, t):
        return {
            "dom": lax.rem(own + s + dom_count, dom_count),
            "band": lax.rem(band + t, band_devices),
        }

    barrier = pltpu.get_barrier_semaphore()
    for s, t in partners:
        pl.semaphore_signal(
            barrier, inc=1, device_id=device(s, t), device_id_type=pl.DeviceIdType.MESH
        )
    pl.semaphore_wait(barrier, len(partners))
    copies = []
    for s, t in partners:
        slot = (s + 1) * band_devices + t
        copy = pltpu.make_async_remote_copy(
            src_ref=part_ref.at[s + 1],
            dst_ref=held_ref.at[slot],
            send_sem=send_sem.at[slot],
            recv_sem=recv_sem.at[slot],
            device_id=device(s, t),
            device_id_type=pl.DeviceIdType.MESH,
        )
        copy.start()
        copies.append((slot, copy))
    total = part_ref[1]
    for slot, copy in copies:
        copy.wait_recv()
        total = total + held_ref[slot]
    for slot, copy in copies:
        copy.wait_send()
    out_ref[...] = total


def edge_kernel(edge_ref, before_ref, after_ref, inner_ref, out_ref):
    side = pl.program_id(1)

    @pl.when(side == 0)
    def _():
        b2 = before_ref[:, 0].astype(F32)
        b1 = before_ref[:, 1].astype(F32)
        out_ref[:, 0] = (edge_ref[:, 0] + (b2 - 16.0 * b1) * (1.0 / 24.0)).astype(BF16)
        out_ref[:, 1] = (edge_ref[:, 1] + b1 * (1.0 / 24.0)).astype(BF16)

    @pl.when(side == 1)
    def _():
        a1 = after_ref[:, 0].astype(F32)
        a2 = after_ref[:, 1].astype(F32)
        out_ref[:, 0] = (edge_ref[:, 0] + a1 * (1.0 / 24.0)).astype(BF16)
        out_ref[:, 1] = (edge_ref[:, 1] + (a2 - 16.0 * a1) * (1.0 / 24.0)).astype(BF16)


def per_device(
    wavefunctions, potential, projectors, margin_atoms, tile_rows, coupling, band_weights
):
    band_count, plane_count, width_y, width_z = wavefunctions.shape
    entry_count, proj_count, tile_len = projectors.shape
    depth = tile_len // width_z
    row_count = plane_count * width_y
    band_pad = max(band_count, ROWS)
    dims = (band_count, band_pad, plane_count, width_y, entry_count, proj_count, depth)
    dom_count = lax.axis_size("dom")
    band_devices = lax.axis_size("band")
    own_index = lax.axis_index("dom")

    up = [(i, (i + 1) % dom_count) for i in range(dom_count)]
    down = [(j, i) for i, j in up]
    before = lax.ppermute(wavefunctions[:, plane_count - 2 :], "dom", up)
    after = lax.ppermute(wavefunctions[:, :2], "dom", down)

    params = pltpu.CompilerParams(vmem_limit_bytes=VMEM_LIMIT)
    swap = jnp.asarray(band_swap(band_count, band_pad), BF16)
    first_z = jnp.asarray(circulant(width_z, {-2: 1.0, -1: -8.0, 1: 8.0, 2: -1.0}), BF16)
    second_z = jnp.asarray(
        circulant(width_z, {-2: -1.0, -1: 16.0, 0: -90.0, 1: 16.0, 2: -1.0}), BF16
    )
    second_y = jnp.asarray(circulant(width_y, {-2: -1.0, -1: 16.0, 1: 16.0, 2: -1.0}), BF16)

    relative = lax.rem(margin_atoms // ATOM_DEV - own_index + 1 + dom_count, dom_count)
    entry_lanes = -(-entry_count * proj_count // LANES) * LANES
    lane = jnp.arange(entry_lanes, dtype=jnp.int32)
    spare = (0, entry_lanes // proj_count - entry_count)
    first_lane = jnp.pad(
        relative * LANES + (margin_atoms % ATOM_DEV) * proj_count, spare, constant_values=-LANES
    )
    pick_lane = jnp.pad(
        relative * LANES + margin_atoms % ATOM_DEV, spare, constant_values=-LANES
    )
    target = jnp.arange(3 * LANES, dtype=jnp.int32)[None, :]
    first_lane = jnp.repeat(first_lane, proj_count) + lane % proj_count
    sort = (first_lane[:, None] == target).astype(BF16)
    pick = (jnp.repeat(pick_lane, proj_count)[:, None] == target).astype(BF16)
    symmetric = 0.5 * (coupling + coupling.T)
    mix = jnp.kron(jnp.eye(LANES // proj_count, dtype=F32), symmetric)
    weights = jnp.pad(-2.0 * band_weights, (0, band_pad - band_count))[:, None]
    flat = projectors.reshape(entry_count * proj_count, tile_len)
    group = LANES // proj_count

    turned, table = pl.pallas_call(
        functools.partial(margin_kernel, dims),
        out_shape=(
            jax.ShapeDtypeStruct((row_count, band_pad, width_z), BF16),
            jax.ShapeDtypeStruct((band_pad, 3 * LANES), BF16),
        ),
        in_specs=[vmem(), vmem(), smem(), vmem(), vmem()],
        out_specs=(vmem(), vmem()),
        scratch_shapes=[
            pltpu.VMEM((group * band_pad, tile_len), BF16),
            pltpu.VMEM((band_pad, entry_lanes), F32),
        ],
        compiler_params=params,
        cost_estimate=pl.CostEstimate(flops=1 << 31, bytes_accessed=9 << 20, transcendentals=0),
        name="margins",
    )(wavefunctions, flat, tile_rows, swap, sort)

    distinct, places, tables = {}, [], []
    for u in range(-2, 3):
        key = u % dom_count
        if key not in distinct:
            distinct[key] = len(tables)
            if key == 0:
                tables.append(table)
            else:
                pairs = [((i + u) % dom_count, i) for i in range(dom_count)]
                tables.append(lax.ppermute(table, "dom", pairs))
        places.append((u, distinct[key]))

    measured = pl.pallas_call(
        functools.partial(gradient_kernel, dims),
        out_shape=jax.ShapeDtypeStruct((3 * band_pad, entry_lanes), F32),
        in_specs=[vmem(), vmem(), smem(), vmem()],
        out_specs=vmem(),
        scratch_shapes=[
            pltpu.VMEM((row_count, 3 * band_pad, width_z), BF16),
            pltpu.VMEM((3 * group * band_pad, tile_len), BF16),
        ],
        compiler_params=params,
        cost_estimate=pl.CostEstimate(flops=1 << 32, bytes_accessed=9 << 20, transcendentals=0),
        name="gradients",
    )(turned, flat, tile_rows, first_z)

    inner, edge, coef = pl.pallas_call(
        functools.partial(apply_kernel, dims, tuple(places_of(places, tables))),
        out_shape=(
            jax.ShapeDtypeStruct(wavefunctions.shape, BF16),
            jax.ShapeDtypeStruct((band_count, 4, width_y, width_z), F32),
            jax.ShapeDtypeStruct((band_pad, entry_lanes), F32),
        ),
        in_specs=[vmem()] * len(places) + [vmem(), vmem(), vmem(), smem()] + [vmem()] * 5,
        out_specs=(vmem(), vmem(), vmem()),
        scratch_shapes=[
            pltpu.VMEM((row_count, band_pad, width_z), F32),
            pltpu.VMEM(wavefunctions.shape, BF16),
        ],
        compiler_params=params,
        cost_estimate=pl.CostEstimate(flops=1 << 32, bytes_accessed=16 << 20, transcendentals=0),
        name="apply",
    )(
        *[tables[index] for _, index in places], wavefunctions, potential, flat, tile_rows, swap,
        sort, mix, second_y, second_z,
    )

    partial = pl.pallas_call(
        functools.partial(force_kernel, dims),
        out_shape=jax.ShapeDtypeStruct((3, 8, LANES), F32),
        in_specs=[vmem(), vmem(), vmem(), smem()] + [vmem()] * 5,
        out_specs=vmem(),
        scratch_shapes=[
            pltpu.VMEM((row_count, band_pad, width_z), BF16),
            pltpu.VMEM((group * band_pad, tile_len), BF16),
            pltpu.VMEM((band_pad, entry_lanes), F32),
        ],
        compiler_params=params,
        cost_estimate=pl.CostEstimate(flops=1 << 30, bytes_accessed=4 << 20, transcendentals=0),
        name="force_part",
    )(before, after, flat, tile_rows, swap, measured, coef, weights, pick)

    slots = 3 * band_devices
    forces = pl.pallas_call(
        functools.partial(reduce_kernel, dom_count, band_devices),
        out_shape=jax.ShapeDtypeStruct((8, LANES), F32),
        in_specs=[vmem()],
        out_specs=vmem(),
        scratch_shapes=[
            pltpu.VMEM((slots, 8, LANES), F32),
            pltpu.SemaphoreType.DMA((slots,)),
            pltpu.SemaphoreType.DMA((slots,)),
        ],
        compiler_params=pltpu.CompilerParams(collective_id=0, has_side_effects=True),
        name="force_sum",
    )(partial)[:3, :ATOM_DEV]

    chunk = max(band_count // 4, 1)
    applied = pl.pallas_call(
        edge_kernel,
        grid=(band_count // chunk, 2),
        out_shape=jax.ShapeDtypeStruct(wavefunctions.shape, BF16),
        in_specs=[
            pl.BlockSpec((chunk, 2, width_y, width_z), lambda i, side: (i, side, 0, 0)),
            pl.BlockSpec((chunk, 2, width_y, width_z), lambda i, side: (i, 0, 0, 0)),
            pl.BlockSpec((chunk, 2, width_y, width_z), lambda i, side: (i, 0, 0, 0)),
            pl.BlockSpec(memory_space=pl.ANY),
        ],
        out_specs=pl.BlockSpec(
            (chunk, 2, width_y, width_z),
            lambda i, side: (i, side * (plane_count // 2 - 1), 0, 0),
        ),
        input_output_aliases={3: 0},
        compiler_params=params,
        cost_estimate=pl.CostEstimate(flops=1 << 24, bytes_accessed=8 << 20, transcendentals=0),
        name="edges",
    )(edge, before, after, inner)
    return (applied, forces)


def places_of(places, tables):
    return [(u, position) for position, (u, _) in enumerate(places)]


def solution(mesh):
    placed = (
        P("band", "dom", None, None),
        P("dom", None, None),
        P("dom", None, None),
        P("dom"),
        P("dom"),
        P(),
        P("band"),
    )
    return jax.shard_map(
        per_device,
        mesh=mesh,
        in_specs=placed,
        out_specs=(P("band", "dom", None, None), P(None, "dom")),
        check_vma=False,
    )
```

profile of v0, /device:TPU:1, one launch (start us, length us, event | category | flops | bytes accessed | tf_op | source)
XLA Modules:
  0.0 76.0 jit_solution(5096279789412437544)
XLA Ops:
  0.6 0.7 fusion.10
  1.3 0.7 multiply_add_fusion
  2.0 0.1 broadcast_in_dim.15
  2.1 0.1 reshape.40
  2.2 0.1 fusion.sort_ref.refs_10_
  2.3 0.0 copy-start.3
  2.3 1.1 %copy-done.3 = bf16[36,8,1024]{2,1,0:T(8,128)(2,1)S(1)} copy-done((bf16[36,8,1024]{2,1,0:T(8,128)(2,1)S(1)}, bf16[36,8,1024]{2,1,0:T(8,128)(2,1)}, u32[]{:S(2)}) %copy-start.3) | copy-done | bytes 589848
  3.4 0.0 copy-start.6
  3.4 0.7 copy-done.6
  4.0 0.0 copy-start.8
  4.0 0.9 %copy-done.8 = bf16[256,256]{1,0:T(8,128)(2,1)S(1)} copy-done((bf16[256,256]{1,0:T(8,128)(2,1)S(1)}, bf16[256,256]{1,0:T(8,128)(2,1)}, u32[]{:S(2)}) %copy-start.8) | copy-done | bytes 131096
  4.9 0.0 copy-start.13
  4.9 0.0 copy-start.14
  4.9 8.2 %margins.1 = (bf16[1024,16,128]{2,1,0:T(8,128)(2,1)}, bf16[16,384]{1,0:T(8,128)(2,1)S(1)}) custom-call(bf16[16,8,128,128]{3,2,1,0:T(8,128)(2,1)} %refs_5_.1, bf16[288,1024]{1,0:T(8,128)(2,1)S(1)} %bitcast.9, s32[36]{0:T(128)S(1)} %copy-done.6, bf16[256,256]{1,0:T(8,128)(2,1)S(1)} %copy-done.8, bf16[384,384]{1,0:T(8,128)(2,1)S(1)} %fusion.sort_ref.refs_10_), custom_call_target="tpu_custom_call" | custom-call | flops 2147483648 | bytes 9437184 | tf_op jit(solution)/shard_map/margins/pallas_call | solution.py:361
  13.1 0.0 copy-start.4
  13.1 0.0 copy-start.7
  13.1 0.0 copy-start.12
  13.1 0.1 collective-permute-start.2
  13.2 2.6 %collective-permute-start.1 = (bf16[16,384]{1,0:T(8,128)(2,1)S(1)}, bf16[16,384]{1,0:T(8,128)(2,1)S(1)}, u32[]{:S(2)}, u32[]{:S(2)}) collective-permute-start(bf16[16,384]{1,0:T(8,128)(2,1)S(1)} %get-tuple-element.7.refs_2_), channel_id=1, source_target_pairs={{24,0},{0,8},{8,16},{16,24},{25,1},{1,9},{9,17},{17,25},{26,2},{2,... | collective-permute-start | bytes 36872 | tf_op jit(solution)/shard_map/ppermute | solution.py:387
  15.8 1.1 %collective-permute-start = (bf16[16,384]{1,0:T(8,128)(2,1)S(1)}, bf16[16,384]{1,0:T(8,128)(2,1)S(1)}, u32[]{:S(2)}, u32[]{:S(2)}) collective-permute-start(bf16[16,384]{1,0:T(8,128)(2,1)S(1)} %get-tuple-element.7.refs_2_), channel_id=1, source_target_pairs={{16,0},{24,8},{0,16},{8,24},{17,1},{25,9},{1,17},{9,25},{18,2},{26... | collective-permute-start | bytes 36872 | tf_op jit(solution)/shard_map/ppermute | solution.py:387
  16.9 0.0 copy-done.13
  16.9 1.6 %fusion.12 = (bf16[16,2,128,128]{3,2,1,0:T(8,128)(2,1)}, bf16[16,2,128,128]{3,2,1,0:T(8,128)(2,1)}) fusion(bf16[16,8,128,128]{3,2,1,0:T(8,128)(2,1)S(1)} %copy-done.13), kind=kLoop, calls=%fused_computation.24 | loop fusion | bytes 4194304 | tf_op jit(solution)/shard_map/slice | solution.py:331
  18.5 0.0 collective-permute-start.4
  18.5 1.7 %collective-permute-start.3 = (bf16[16,2,128,128]{3,2,1,0:T(8,128)(2,1)}, bf16[16,2,128,128]{3,2,1,0:T(8,128)(2,1)S(1)}, u32[]{:S(2)}, u32[]{:S(2)}) collective-permute-start(bf16[16,2,128,128]{3,2,1,0:T(8,128)(2,1)} %get-tuple-element.15), channel_id=1, source_target_pairs={{0,8},{8,16},{16,24},{24,0},{1,9},{9,17},{17,25},{25,1},{2,10},{10... | collective-permute-start | bytes 3145736 | tf_op jit(solution)/shard_map/ppermute | solution.py:330
  20.2 0.0 copy-done.14
  20.2 0.1 copy.16
  20.3 0.1 broadcast_in_dim.17
  20.4 0.1 eq.44
  20.5 1.1 %broadcast_multiply_fusion = f32[16,8,16,8]{3,2,1,0:T(8,128)} fusion(f32[8,8]{1,0:T(8,128)S(1)} %fusion.3, f32[16,16]{1,0:T(8,128)S(1)} %fusion.2), kind=kLoop, calls=%fused_computation.4 | loop fusion | flops 16384 | bytes 66816 | tf_op jit(solution)/shard_map/jit(kron)/mul | solution.py:356
  21.6 0.1 fusion.1.pick_ref
  21.7 0.0 copy-done.4
  21.7 0.0 copy-done.7
  21.8 0.0 copy-done.12
  21.8 0.0 copy-start.15
  21.8 0.0 copy-start.5
  21.8 0.0 copy-start.9
  21.8 0.0 copy-start.10
  21.8 0.0 copy-start.11
  21.8 9.2 %gradients.1.meas_ref = f32[48,384]{1,0:T(8,128)S(1)} custom-call(bf16[1024,16,128]{2,1,0:T(8,128)(2,1)} %get-tuple-element.10.turned_ref, bf16[288,1024]{1,0:T(8,128)(2,1)S(1)} %bitcast.10, s32[36]{0:T(128)S(1)} %copy-done.7, bf16[128,128]{1,0:T(8,128)(2,1)S(1)} %copy-done.12), custom_call_target="tpu_custom_call" | custom-call | flops 4294967296 | bytes 9437184 | tf_op jit(solution)/shard_map/gradients/pallas_call | solution.py:390
  31.1 0.0 copy-done.15
  31.1 0.1 copy.17.weight_ref
  31.2 1.7 %mul.51.refs_11_ = f32[128,128]{1,0:T(8,128)S(1)} reshape(f32[16,8,16,8]{3,2,1,0:T(8,128)} %broadcast_multiply_fusion) | data formatting | bytes 131072 | tf_op jit(solution)/shard_map/jit(kron)/mul | solution.py:356
  32.8 0.0 collective-permute-done.2.refs_3_
  32.8 0.0 collective-permute-done.1.refs_1_
  32.9 0.0 collective-permute-done.refs_0_.refs_4_
  32.9 0.0 copy-done.5
  32.9 0.0 copy-done.9
  32.9 0.0 copy-done.10
  32.9 0.0 copy-done.11
  32.9 17.9 %apply.1 = (bf16[16,8,128,128]{3,2,1,0:T(8,128)(2,1)}, f32[16,4,128,128]{3,2,1,0:T(8,128)}, f32[16,384]{1,0:T(8,128)S(1)}) custom-call(bf16[16,384]{1,0:T(8,128)(2,1)S(1)} %collective-permute-done.refs_0_.refs_4_, bf16[16,384]{1,0:T(8,128)(2,1)S(1)} %collective-permute-done.1.refs_1_, bf16[16,384]{1,0:T(8,128)(2,1)S(1)} %get-tuple-element.7.refs_2_, ...), custom_call_target="tpu_custom_call" | custom-call | flops 4294967296 | bytes 16777216 | tf_op jit(solution)/shard_map/apply/pallas_call | solution.py:404
  50.8 0.0 collective-permute-done.4.after_ref
  50.8 0.0 collective-permute-done.3.before_ref
  50.8 0.0 copy-start
  50.8 1.0 %copy-done = bf16[16,2,128,128]{3,2,1,0:T(8,128)(2,1)} copy-done((bf16[16,2,128,128]{3,2,1,0:T(8,128)(2,1)}, bf16[16,2,128,128]{3,2,1,0:T(8,128)(2,1)S(1)}, u32[]{:S(2)}) %copy-start) | copy-done | bytes 1048600
  51.8 5.3 %force_part.1.part_ref = f32[3,8,128]{2,1,0:T(8,128)S(1)} custom-call(bf16[16,2,128,128]{3,2,1,0:T(8,128)(2,1)} %copy-done, bf16[16,2,128,128]{3,2,1,0:T(8,128)(2,1)} %collective-permute-done.4.after_ref, bf16[288,1024]{1,0:T(8,128)(2,1)S(1)} %bitcast.12, s32[36]{0:T(128)S(1)} %copy-done.7, bf16[256,256]{1,0:T(8,128)(2,1)S(1)} %copy-done.9, ...), custom_call_target="tpu_custom_call" | custom-call | flops 1073741824 | bytes 4194304 | tf_op jit(solution)/shard_map/force_part/pallas_call | solution.py:425
  57.1 0.0 copy-start.2
  57.1 0.6 copy-done.2
  57.7 9.2 %force_sum.1 = f32[8,128]{1,0:T(8,128)} custom-call(f32[3,8,128]{2,1,0:T(8,128)} %copy-done.2), custom_call_target="tpu_custom_call" | custom-call | tf_op jit(solution)/shard_map/force_sum/pallas_call | solution.py:441
  66.9 1.3 %slice.11 = f32[3,12]{1,0:T(4,128)} slice(f32[8,128]{1,0:T(8,128)} %force_sum.1), slice={[0:3], [0:12]} | slice | bytes 288 | tf_op jit(solution)/shard_map/slice | solution.py:441
  68.2 0.0 copy-start.1
  68.2 1.2 %copy-done.1 = bf16[16,2,128,128]{3,2,1,0:T(8,128)(2,1)S(1)} copy-done((bf16[16,2,128,128]{3,2,1,0:T(8,128)(2,1)S(1)}, bf16[16,2,128,128]{3,2,1,0:T(8,128)(2,1)}, u32[]{:S(2)}) %copy-start.1) | copy-done | bytes 1048600
  69.4 6.6 %edges.1 = bf16[16,8,128,128]{3,2,1,0:T(8,128)(2,1)} custom-call(f32[16,4,128,128]{3,2,1,0:T(8,128)} %get-tuple-element.8.edge_ref, bf16[16,2,128,128]{3,2,1,0:T(8,128)(2,1)S(1)} %copy-done.1, bf16[16,2,128,128]{3,2,1,0:T(8,128)(2,1)} %collective-permute-done.4.after_ref, ...), custom_call_target="tpu_custom_call", output_to_operand_aliasing={{}: (3, {})} | custom-call | flops 16777216 | bytes 8388608 | tf_op jit(solution)/shard_map/edges/pallas_call | solution.py:456
  (6 shorter events, 0.0 us)
Async XLA Ops:
  2.3 1.1 %copy-start.3 = (bf16[36,8,1024]{2,1,0:T(8,128)(2,1)S(1)}, bf16[36,8,1024]{2,1,0:T(8,128)(2,1)}, u32[]{:S(2)}) copy-start(bf16[36,8,1024]{2,1,0:T(8,128)(2,1)} %param.13) | copy-start | bytes 1769476
  3.4 0.7 copy-start.6
  4.0 0.9 %copy-start.8 = (bf16[256,256]{1,0:T(8,128)(2,1)S(1)}, bf16[256,256]{1,0:T(8,128)(2,1)}, u32[]{:S(2)}) copy-start(bf16[256,256]{1,0:T(8,128)(2,1)} %constant.68.clone.swap_ref.refs_9_) | copy-start | bytes 393220
  4.9 12.0 %copy-start.13 = (bf16[16,8,128,128]{3,2,1,0:T(8,128)(2,1)S(1)}, bf16[16,8,128,128]{3,2,1,0:T(8,128)(2,1)}, u32[]{:S(2)}) copy-start(bf16[16,8,128,128]{3,2,1,0:T(8,128)(2,1)} %refs_5_.1) | copy-start | bytes 12582916
  4.9 15.3 %copy-start.14 = (f32[8,8]{1,0:T(8,128)S(1)}, f32[8,8]{1,0:T(8,128)}, u32[]{:S(2)}) copy-start(f32[8,8]{1,0:T(8,128)} %param.16) | copy-start | bytes 772
  13.1 8.7 %copy-start.4 = (bf16[36,8,1024]{2,1,0:T(8,128)(2,1)S(1)}, bf16[36,8,1024]{2,1,0:T(8,128)(2,1)}, u32[]{:S(2)}) copy-start(bf16[36,8,1024]{2,1,0:T(8,128)(2,1)} %param.13) | copy-start | bytes 1769476
  13.1 8.7 %copy-start.7 = (s32[36]{0:T(128)S(1)}, s32[36]{0:T(128)}, u32[]{:S(2)}) copy-start(s32[36]{0:T(128)} %rows_ref.5) | copy-start | bytes 436
  13.1 8.7 %copy-start.12 = (bf16[128,128]{1,0:T(8,128)(2,1)S(1)}, bf16[128,128]{1,0:T(8,128)(2,1)}, u32[]{:S(2)}) copy-start(bf16[128,128]{1,0:T(8,128)(2,1)} %constant.69.clone.first_ref) | copy-start | bytes 98308
  13.1 19.8 %collective-permute-start.2 = (bf16[16,384]{1,0:T(8,128)(2,1)S(1)}, bf16[16,384]{1,0:T(8,128)(2,1)S(1)}, u32[]{:S(2)}, u32[]{:S(2)}) collective-permute-start(bf16[16,384]{1,0:T(8,128)(2,1)S(1)} %get-tuple-element.7.refs_2_), channel_id=1, source_target_pairs={{8,0},{16,8},{24,16},{0,24},{9,1},{17,9},{25,17},{1,25},{10,2},{18... | collective-permute-start | bytes 36872 | tf_op jit(solution)/shard_map/ppermute | solution.py:387
  13.2 19.7 %collective-permute-start.1 = (bf16[16,384]{1,0:T(8,128)(2,1)S(1)}, bf16[16,384]{1,0:T(8,128)(2,1)S(1)}, u32[]{:S(2)}, u32[]{:S(2)}) collective-permute-start(bf16[16,384]{1,0:T(8,128)(2,1)S(1)} %get-tuple-element.7.refs_2_), channel_id=1, source_target_pairs={{24,0},{0,8},{8,16},{16,24},{25,1},{1,9},{9,17},{17,25},{26,2},{2,... | collective-permute-start | bytes 36872 | tf_op jit(solution)/shard_map/ppermute | solution.py:387
  15.8 17.1 %collective-permute-start = (bf16[16,384]{1,0:T(8,128)(2,1)S(1)}, bf16[16,384]{1,0:T(8,128)(2,1)S(1)}, u32[]{:S(2)}, u32[]{:S(2)}) collective-permute-start(bf16[16,384]{1,0:T(8,128)(2,1)S(1)} %get-tuple-element.7.refs_2_), channel_id=1, source_target_pairs={{16,0},{24,8},{0,16},{8,24},{17,1},{25,9},{1,17},{9,25},{18,2},{26... | collective-permute-start | bytes 36872 | tf_op jit(solution)/shard_map/ppermute | solution.py:387
  18.5 32.3 %collective-permute-start.4 = (bf16[16,2,128,128]{3,2,1,0:T(8,128)(2,1)}, bf16[16,2,128,128]{3,2,1,0:T(8,128)(2,1)}, u32[]{:S(2)}, u32[]{:S(2)}) collective-permute-start(bf16[16,2,128,128]{3,2,1,0:T(8,128)(2,1)} %get-tuple-element.14), channel_id=1, source_target_pairs={{8,0},{16,8},{24,16},{0,24},{9,1},{17,9},{25,17},{1,25},{10,2},{18... | collective-permute-start | bytes 3145736 | tf_op jit(solution)/shard_map/ppermute | solution.py:331
  18.5 32.3 %collective-permute-start.3 = (bf16[16,2,128,128]{3,2,1,0:T(8,128)(2,1)}, bf16[16,2,128,128]{3,2,1,0:T(8,128)(2,1)S(1)}, u32[]{:S(2)}, u32[]{:S(2)}) collective-permute-start(bf16[16,2,128,128]{3,2,1,0:T(8,128)(2,1)} %get-tuple-element.15), channel_id=1, source_target_pairs={{0,8},{8,16},{16,24},{24,0},{1,9},{9,17},{17,25},{25,1},{2,10},{10... | collective-permute-start | bytes 3145736 | tf_op jit(solution)/shard_map/ppermute | solution.py:330
  21.8 9.3 %copy-start.15 = (f32[16]{0:T(128)S(1)}, f32[16]{0:T(128)}, u32[]{:S(2)}) copy-start(f32[16]{0:T(128)} %param.17) | copy-start | bytes 196
  21.8 11.1 %copy-start.5 = (f32[8,128,128]{2,1,0:T(8,128)S(1)}, f32[8,128,128]{2,1,0:T(8,128)}, u32[]{:S(2)}) copy-start(f32[8,128,128]{2,1,0:T(8,128)} %refs_6_.1) | copy-start | bytes 1572868
  21.8 11.1 %copy-start.9 = (bf16[256,256]{1,0:T(8,128)(2,1)S(1)}, bf16[256,256]{1,0:T(8,128)(2,1)}, u32[]{:S(2)}) copy-start(bf16[256,256]{1,0:T(8,128)(2,1)} %constant.68.clone.swap_ref.refs_9_) | copy-start | bytes 393220
  21.8 11.1 %copy-start.10 = (bf16[128,128]{1,0:T(8,128)(2,1)S(1)}, bf16[128,128]{1,0:T(8,128)(2,1)}, u32[]{:S(2)}) copy-start(bf16[128,128]{1,0:T(8,128)(2,1)} %constant.71.clone.refs_12_) | copy-start | bytes 98308
  21.8 11.1 %copy-start.11 = (bf16[128,128]{1,0:T(8,128)(2,1)S(1)}, bf16[128,128]{1,0:T(8,128)(2,1)}, u32[]{:S(2)}) copy-start(bf16[128,128]{1,0:T(8,128)(2,1)} %constant.70.clone.refs_13_) | copy-start | bytes 98308
  50.8 1.0 %copy-start = (bf16[16,2,128,128]{3,2,1,0:T(8,128)(2,1)}, bf16[16,2,128,128]{3,2,1,0:T(8,128)(2,1)S(1)}, u32[]{:S(2)}) copy-start(bf16[16,2,128,128]{3,2,1,0:T(8,128)(2,1)S(1)} %collective-permute-done.3.before_ref) | copy-start | bytes 3145732
  57.1 0.6 copy-start.2
  68.2 1.2 %copy-start.1 = (bf16[16,2,128,128]{3,2,1,0:T(8,128)(2,1)S(1)}, bf16[16,2,128,128]{3,2,1,0:T(8,128)(2,1)}, u32[]{:S(2)}) copy-start(bf16[16,2,128,128]{3,2,1,0:T(8,128)(2,1)} %copy-done) | copy-start | bytes 3145732
where the time goes:
time: 76.6 us; the launch traced here: 76 us
  Pallas kernels  56.4 us (74%)
  local copies, waits for them, and re-layouts  10.5 us (14%)
  starting transfers between devices  5.53 us (7%)
  other arithmetic  2.74 us (4%)
  between operations  0.85 us (1%)
    pallas_call x1, Pallas kernels, per_device(): pl.pallas_call(functools.partial(apply_kernel, dims, tuple(places_of(plac...  17.9 us
    pallas_call x1, Pallas kernels, per_device(): pl.pallas_call(functools.partial(gradient_kernel, dims), out_shape=jax.Sh...  9.25 us
    pallas_call x1, Pallas kernels, per_device(): pl.pallas_call(functools.partial(reduce_kernel, dom_count, band_devices),...  9.23 us
    pallas_call x1, Pallas kernels, per_device(): pl.pallas_call(functools.partial(margin_kernel, dims), out_shape=(jax.Sha...  8.16 us
    pallas_call x1, Pallas kernels, per_device(): pl.pallas_call(edge_kernel, grid=(band_count // chunk, 2), out_shape=jax....  6.57 us
    unnamed x33, local copies, waits for them, and re-layouts  5.56 us
    pallas_call x1, Pallas kernels, per_device(): pl.pallas_call(functools.partial(force_kernel, dims), out_shape=jax.Shape...  5.26 us
    ppermute x3, starting transfers between devices, per_device(): tables.append(lax.ppermute(table, 'dom', pairs))  3.79 us
  transfers between devices with their start and end apart: 5, of which 0 were waited for; matrix products, arithmetic and copies ran while one was open for 6% of the time, Pallas kernels for 36%

commit v1 on v0

v1 whole, which is shorter than its diff:
```python
import functools

import jax
import jax.numpy as jnp
import numpy as np
from jax import lax
from jax.experimental import pallas as pl
from jax.experimental.pallas import tpu as pltpu
from jax.sharding import PartitionSpec as P

ATOM_DEV = 12
LANES = 128
ROWS = 16
VMEM_LIMIT = 52 * 1024 * 1024
F32 = jnp.float32
BF16 = jnp.bfloat16
HIGHEST = lax.Precision.HIGHEST
SMALL = pl.CostEstimate(flops=1 << 20, bytes_accessed=1 << 12, transcendentals=0)


def vmem():
    return pl.BlockSpec(memory_space=pltpu.VMEM)


def smem():
    return pl.BlockSpec(memory_space=pltpu.SMEM)


def dot(a, b):
    return jnp.dot(a, b, preferred_element_type=F32)


def dot_nt(a, b, precision=None):
    return lax.dot_general(
        a, b, (((1,), (1,)), ((), ())), precision=precision, preferred_element_type=F32
    )


def circulant(width, taps):
    table = np.zeros((width, width), np.float32)
    for offset, value in taps.items():
        for target in range(width):
            table[(target + offset) % width, target] += value
    return table


def band_swap(band_count, band_pad):
    table = np.zeros((ROWS * band_pad, band_count * ROWS), np.float32)
    for y in range(ROWS):
        for b in range(band_count):
            table[y * band_pad + b, b * ROWS + y] = 1.0
    return table


def pick_groups(whole, count, height, proj_count):
    width = count * proj_count
    whole = whole.reshape(count, height, width)
    lane = lax.broadcasted_iota(jnp.int32, (count, height, width), 2) // proj_count
    item = lax.broadcasted_iota(jnp.int32, (count, height, width), 0)
    return jnp.sum(jnp.where(lane == item, whole, 0.0), axis=0)


def turn_pair(swap, left, right):
    return dot(swap, jnp.concatenate([left, right], axis=1)).astype(BF16)


def signal_all(devices):
    barrier = pltpu.get_barrier_semaphore()
    for device in devices:
        pl.semaphore_signal(
            barrier, inc=1, device_id=device, device_id_type=pl.DeviceIdType.MESH
        )


def wait_all(devices):
    pl.semaphore_wait(pltpu.get_barrier_semaphore(), len(devices))


def margin_kernel(
    dims, dom_count, wave_ref, proj_ref, rows_ref, swap_ref, sort_ref, first_ref, tables_ref,
    meas_ref, turned_ref, proj_z_ref, lhs_ref, both_ref, own_ref, held_ref, send_sem, recv_sem,
):
    band_count, band_pad, plane_count, width_y, entry_count, proj_count, depth = dims
    stride = width_y + 4
    group = LANES // proj_count
    own = lax.axis_index("dom")
    moves = other_moves(dom_count)
    signal_all([{"dom": lax.rem(own + u, dom_count)} for u in moves])

    turned_ref[: 2 * stride] = jnp.zeros((2 * stride, band_pad, LANES), BF16)
    turned_ref[(plane_count + 2) * stride :] = jnp.zeros((2 * stride, band_pad, LANES), BF16)

    def turn(step, carry):
        rows = pl.ds(pl.multiple_of(step * ROWS, ROWS), ROWS)
        for x in range(0, plane_count, 2):
            moved = turn_pair(
                swap_ref[...],
                wave_ref[:, x, rows, :].reshape(band_count * ROWS, LANES),
                wave_ref[:, x + 1, rows, :].reshape(band_count * ROWS, LANES),
            )
            for k in range(2):
                turned_ref[pl.ds((x + k + 2) * stride + 2 + step * ROWS, ROWS)] = moved[
                    :, k * LANES : (k + 1) * LANES
                ].reshape(ROWS, band_pad, LANES)
        return carry

    lax.fori_loop(0, width_y // ROWS, turn, 0)
    for x in range(2, plane_count + 2):
        base = x * stride
        turned_ref[base : base + 2] = turned_ref[base + width_y : base + width_y + 2]
        turned_ref[base + width_y + 2 : base + width_y + 4] = turned_ref[base + 2 : base + 4]

    for j in range(depth):
        columns = slice(j * LANES, (j + 1) * LANES)
        proj_z_ref[:, columns] = (
            dot(proj_ref[:, columns], first_ref[...]) * (-1.0 / 12.0)
        ).astype(BF16)

    def place(row, j):
        at = row + j
        return at + 4 * lax.div(at, width_y) + 2 * stride + 2

    meas_ref[...] = jnp.zeros_like(meas_ref)
    both_ref[...] = jnp.zeros_like(both_ref)
    for start in range(0, entry_count, group):
        count = min(group, entry_count - start)
        width = count * proj_count
        first = start * proj_count

        def fetch(k, carry):
            row = rows_ref[start + k]
            for j in range(depth):
                lhs_ref[k, :band_pad, j * LANES : (j + 1) * LANES] = turned_ref[place(row, j)]
            return carry

        lax.fori_loop(0, count, fetch, 0)
        lhs = lhs_ref[:count, :band_pad].reshape(count * band_pad, depth * LANES)
        whole = dot_nt(lhs, proj_ref[first : first + width])
        both_ref[:, first : first + width] = pick_groups(whole, count, band_pad, proj_count)
        whole = dot_nt(lhs, proj_z_ref[first : first + width])
        meas_ref[2 * band_pad :, first : first + width] = pick_groups(
            whole, count, band_pad, proj_count
        )

    own_ref[...] = dot(both_ref[...].astype(BF16), sort_ref[...]).astype(BF16)
    wait_all(moves)
    copies = []
    for slot, u in enumerate(moves):
        copy = pltpu.make_async_remote_copy(
            src_ref=own_ref,
            dst_ref=held_ref.at[slot],
            send_sem=send_sem.at[slot],
            recv_sem=recv_sem.at[slot],
            device_id={"dom": lax.rem(own + dom_count - u, dom_count)},
            device_id_type=pl.DeviceIdType.MESH,
        )
        copy.start()
        copies.append(copy)

    for start in range(0, entry_count, group):
        count = min(group, entry_count - start)
        width = count * proj_count
        first = start * proj_count

        def derive(k, carry):
            row = rows_ref[start + k]
            for j in range(depth):
                at = place(row, j)
                columns = slice(j * LANES, (j + 1) * LANES)
                for part, step in ((0, stride), (1, 1)):
                    far = turned_ref[at - 2 * step].astype(F32) - turned_ref[
                        at + 2 * step
                    ].astype(F32)
                    near = turned_ref[at + step].astype(F32) - turned_ref[at - step].astype(F32)
                    lhs_ref[k, part * band_pad : (part + 1) * band_pad, columns] = (
                        far * (1.0 / 12.0) + near * (2.0 / 3.0)
                    ).astype(BF16)
            return carry

        lax.fori_loop(0, count, derive, 0)
        lhs = lhs_ref[:count].reshape(count * 2 * band_pad, depth * LANES)
        whole = dot_nt(lhs, proj_ref[first : first + width])
        meas_ref[: 2 * band_pad, first : first + width] = pick_groups(
            whole, count, 2 * band_pad, proj_count
        )

    tables_ref[0] = own_ref[...]
    for slot, copy in enumerate(copies):
        copy.wait_recv()
        tables_ref[slot + 1] = held_ref[slot]
    for copy in copies:
        copy.wait_send()


def apply_kernel(
    dims, places, tables_ref, wave_ref, pot_ref, proj_ref, rows_ref, back_ref, sort_ref, mix_ref,
    second_y_ref, second_z_ref, out_ref, edge_ref, coef_ref, acc_ref, part_ref, scale_ref,
    inner_buf, edge_buf, inner_sem, edge_sem,
):
    band_count, band_pad, plane_count, width_y, entry_count, proj_count, depth = dims
    totals = []
    for s in (-1, 0, 1):
        total = jnp.zeros((band_pad, LANES), F32)
        for u in (s - 1, s, s + 1):
            block = s - u + 1
            held = tables_ref[places[u], :, block * LANES : (block + 1) * LANES]
            total = total + held.astype(F32)
        totals.append(total)
    scaled = jnp.dot(
        jnp.concatenate(totals, axis=0), mix_ref[...], precision=HIGHEST,
        preferred_element_type=F32,
    )
    scaled = jnp.concatenate(
        [scaled[s * band_pad : (s + 1) * band_pad] for s in range(3)], axis=1
    )
    high = scaled.astype(BF16)
    low = (scaled - high.astype(F32)).astype(BF16)
    sorted_back = dot(jnp.concatenate([high, low], axis=0), sort_ref[...])
    half = sorted_back[:band_pad]
    coef_ref[...] = half + sorted_back[band_pad:]

    acc_ref[...] = jnp.zeros_like(acc_ref)
    group = LANES // proj_count
    for start in range(0, entry_count, group):
        count = min(group, entry_count - start)
        width = count * proj_count
        first = start * proj_count
        held = jnp.broadcast_to(half[:, first : first + width][None], (count, band_pad, width))
        lane = lax.broadcasted_iota(jnp.int32, (count, band_pad, width), 2) // proj_count
        item = lax.broadcasted_iota(jnp.int32, (count, band_pad, width), 0)
        spread = jnp.where(lane == item, held, 0.0).reshape(count * band_pad, width).astype(BF16)
        for j in range(depth):
            terms = dot(spread, proj_ref[first : first + width, j * LANES : (j + 1) * LANES])
            for k in range(count):
                row = rows_ref[start + k] + j
                acc_ref[row] += terms[k * band_pad : (k + 1) * band_pad]

    def turn_back(step, carry):
        rows = pl.ds(pl.multiple_of(step * ROWS, ROWS), ROWS)
        for x in range(0, plane_count, 2):
            blocks = [
                (acc_ref[pl.ds((x + k) * width_y + step * ROWS, ROWS)] * -24.0)
                .astype(BF16)
                .reshape(ROWS * band_pad, LANES)
                for k in range(2)
            ]
            moved = turn_pair(back_ref[...], *blocks)
            for k in range(2):
                part_ref[:, x + k, rows, :] = moved[:, k * LANES : (k + 1) * LANES].reshape(
                    band_count, ROWS, LANES
                )
        return carry

    lax.fori_loop(0, width_y // ROWS, turn_back, 0)
    scale_ref[...] = (pot_ref[...] * -24.0).astype(BF16)

    def inner_copy(b):
        return pltpu.make_async_copy(
            inner_buf.at[b], out_ref.at[b, pl.ds(2, plane_count - 4)], inner_sem.at[b]
        )

    def edge_copy(b):
        return pltpu.make_async_copy(edge_buf.at[b], edge_ref.at[b], edge_sem.at[b])

    def each_pair(pair, carry):
        for x in range(plane_count):
            tops, adds = [], []
            for k in range(2):
                b = pair * 2 + k

                def near(offset):
                    return [
                        wave_ref[b, x + o]
                        for o in (offset, -offset)
                        if 0 <= x + o < plane_count
                    ]

                here = wave_ref[b, x]
                one, two = near(1), near(2)
                side = sum(one[1:], one[0]) * jnp.asarray(16.0, BF16)
                side = side - sum(two[1:], two[0])
                adds.append(side + (scale_ref[x] * here + part_ref[b, x]))
                tops.append(here)
            both = jnp.concatenate(
                [jnp.concatenate(tops, axis=1), jnp.concatenate(adds, axis=1)], axis=0
            )
            lap = dot(second_y_ref[...], both)
            along_z = dot(jnp.concatenate(tops, axis=0), second_z_ref[...])
            for k in range(2):
                b = pair * 2 + k
                total = lap[:, k * LANES : (k + 1) * LANES]
                total = total + along_z[k * width_y : (k + 1) * width_y]
                total = total * (-1.0 / 24.0)
                if x < 2:
                    edge_buf[b, x] = total
                elif x >= plane_count - 2:
                    edge_buf[b, x - plane_count + 4] = total
                else:
                    inner_buf[b, x - 2] = total.astype(BF16)
        for k in range(2):
            inner_copy(pair * 2 + k).start()
            edge_copy(pair * 2 + k).start()
        return carry

    lax.fori_loop(0, band_count // 2, each_pair, 0)

    def finish(b, carry):
        inner_copy(b).wait()
        edge_copy(b).wait()
        return carry

    lax.fori_loop(0, band_count, finish, 0)


def force_kernel(
    dims, dom_count, band_devices, before_ref, after_ref, proj_ref, rows_ref, swap_ref, meas_ref,
    coef_ref, weight_ref, pick_ref, out_ref, field_ref, lhs_ref, extra_ref, part_ref, held_ref,
    send_sem, recv_sem,
):
    band_count, band_pad, plane_count, width_y, entry_count, proj_count, depth = dims
    group = LANES // proj_count
    own = lax.axis_index("dom")
    band = lax.axis_index("band")
    partners = [
        (s, t) for t in range(band_devices) for s in (-1, 0, 1) if (s, t) != (0, 0)
    ]

    def device(s, t):
        return {
            "dom": lax.rem(own + s + dom_count, dom_count),
            "band": lax.rem(band + t, band_devices),
        }

    signal_all([device(s, t) for s, t in partners])

    inner = (plane_count - 4) * width_y
    field_ref[2 * width_y : 2 * width_y + inner] = jnp.zeros((inner, band_pad, LANES), BF16)

    def step_rows(step, carry):
        rows = pl.ds(pl.multiple_of(step * ROWS, ROWS), ROWS)
        b2 = before_ref[:, 0, rows, :].astype(F32)
        b1 = before_ref[:, 1, rows, :].astype(F32)
        a1 = after_ref[:, 0, rows, :].astype(F32)
        a2 = after_ref[:, 1, rows, :].astype(F32)
        last = plane_count - 1
        for x, left, right in ((0, b2 - 8.0 * b1, b1), (last - 1, -a1, 8.0 * a1 - a2)):
            moved = turn_pair(
                swap_ref[...],
                *[
                    (value * (1.0 / 12.0)).astype(BF16).reshape(band_count * ROWS, LANES)
                    for value in (left, right)
                ],
            )
            for k in range(2):
                field_ref[pl.ds((x + k) * width_y + step * ROWS, ROWS)] = moved[
                    :, k * LANES : (k + 1) * LANES
                ].reshape(ROWS, band_pad, LANES)
        return carry

    lax.fori_loop(0, width_y // ROWS, step_rows, 0)
    extra_ref[...] = jnp.zeros_like(extra_ref)
    for start in range(0, entry_count, group):
        count = min(group, entry_count - start)
        width = count * proj_count
        first = start * proj_count

        def fetch(k, carry):
            tile = field_ref[pl.ds(rows_ref[start + k], depth)]
            for j in range(depth):
                lhs_ref[k, :, j * LANES : (j + 1) * LANES] = tile[j]
            return carry

        lax.fori_loop(0, count, fetch, 0)
        lhs = lhs_ref[:count].reshape(count * band_pad, depth * LANES)
        whole = dot_nt(lhs, proj_ref[first : first + width])
        extra_ref[:, first : first + width] = pick_groups(whole, count, band_pad, proj_count)

    weighted = coef_ref[...] * weight_ref[...]
    sums = []
    for k in range(3):
        held = meas_ref[k * band_pad : (k + 1) * band_pad]
        if k == 0:
            held = held + extra_ref[...]
        sums.append(jnp.sum(weighted * held, axis=0, keepdims=True))
    sums = jnp.concatenate(sums + [jnp.zeros((5, sums[0].shape[1]), F32)], axis=0)
    high = sums.astype(BF16)
    rest = sums - high.astype(F32)
    middle = rest.astype(BF16)
    low = (rest - middle.astype(F32)).astype(BF16)
    pieces = jnp.concatenate([high, middle, low, jnp.zeros_like(low)], axis=0)
    spread = dot(pieces, pick_ref[...])
    spread = spread[:8] + spread[8:16] + spread[16:24]
    for s in range(3):
        part_ref[s] = spread[:, s * LANES : (s + 1) * LANES]

    wait_all(partners)
    copies = []
    for s, t in partners:
        slot = (s + 1) * band_devices + t
        copy = pltpu.make_async_remote_copy(
            src_ref=part_ref.at[s + 1],
            dst_ref=held_ref.at[slot],
            send_sem=send_sem.at[slot],
            recv_sem=recv_sem.at[slot],
            device_id=device(s, t),
            device_id_type=pl.DeviceIdType.MESH,
        )
        copy.start()
        copies.append((slot, copy))
    total = part_ref[1]
    for slot, copy in copies:
        copy.wait_recv()
        total = total + held_ref[slot]
    for slot, copy in copies:
        copy.wait_send()
    out_ref[...] = total


def edge_kernel(edge_ref, before_ref, after_ref, inner_ref, out_ref):
    side = pl.program_id(1)

    @pl.when(side == 0)
    def _():
        b2 = before_ref[:, 0].astype(F32)
        b1 = before_ref[:, 1].astype(F32)
        out_ref[:, 0] = (edge_ref[:, 0] + (b2 - 16.0 * b1) * (1.0 / 24.0)).astype(BF16)
        out_ref[:, 1] = (edge_ref[:, 1] + b1 * (1.0 / 24.0)).astype(BF16)

    @pl.when(side == 1)
    def _():
        a1 = after_ref[:, 0].astype(F32)
        a2 = after_ref[:, 1].astype(F32)
        out_ref[:, 0] = (edge_ref[:, 0] + a1 * (1.0 / 24.0)).astype(BF16)
        out_ref[:, 1] = (edge_ref[:, 1] + (a2 - 16.0 * a1) * (1.0 / 24.0)).astype(BF16)


def per_device(
    wavefunctions, potential, projectors, margin_atoms, tile_rows, coupling, band_weights
):
    band_count, plane_count, width_y, width_z = wavefunctions.shape
    entry_count, proj_count, tile_len = projectors.shape
    depth = tile_len // width_z
    row_count = plane_count * width_y
    band_pad = max(band_count, ROWS)
    dims = (band_count, band_pad, plane_count, width_y, entry_count, proj_count, depth)
    dom_count = lax.axis_size("dom")
    band_devices = lax.axis_size("band")
    own_index = lax.axis_index("dom")

    up = [(i, (i + 1) % dom_count) for i in range(dom_count)]
    down = [(j, i) for i, j in up]
    before = lax.ppermute(wavefunctions[:, plane_count - 2 :], "dom", up)
    after = lax.ppermute(wavefunctions[:, :2], "dom", down)

    params = pltpu.CompilerParams(vmem_limit_bytes=VMEM_LIMIT)
    swap = jnp.asarray(band_swap(band_count, band_pad), BF16)
    back = jnp.asarray(band_swap(band_count, band_pad).T, BF16)
    first_z = jnp.asarray(circulant(width_z, {-2: 1.0, -1: -8.0, 1: 8.0, 2: -1.0}), BF16)
    second_z = jnp.asarray(
        circulant(width_z, {-2: -1.0, -1: 16.0, 0: -90.0, 1: 16.0, 2: -1.0}), BF16
    )
    second_y = circulant(width_y, {-2: -1.0, -1: 16.0, 1: 16.0, 2: -1.0})
    second_y = jnp.asarray(
        np.concatenate([second_y, np.eye(width_y, dtype=np.float32)], axis=1), BF16
    )

    relative = lax.rem(margin_atoms // ATOM_DEV - own_index + 1 + dom_count, dom_count)
    entry_lanes = -(-entry_count * proj_count // LANES) * LANES
    lane = jnp.arange(entry_lanes, dtype=jnp.int32)
    spare = (0, entry_lanes // proj_count - entry_count)
    first_lane = jnp.pad(
        relative * LANES + (margin_atoms % ATOM_DEV) * proj_count, spare, constant_values=-LANES
    )
    pick_lane = jnp.pad(
        relative * LANES + margin_atoms % ATOM_DEV, spare, constant_values=-LANES
    )
    target = jnp.arange(3 * LANES, dtype=jnp.int32)[None, :]
    first_lane = jnp.repeat(first_lane, proj_count) + lane % proj_count
    sort = (first_lane[:, None] == target).astype(BF16)
    sort_back = (target.T == first_lane[None, :]).astype(BF16)
    pick = (jnp.repeat(pick_lane, proj_count)[:, None] == target).astype(BF16)
    symmetric = 0.5 * (coupling + coupling.T)
    mix = jnp.kron(jnp.eye(LANES // proj_count, dtype=F32), symmetric)
    weights = jnp.pad(-2.0 * band_weights, (0, band_pad - band_count))[:, None]
    flat = projectors.reshape(entry_count * proj_count, tile_len)
    group = LANES // proj_count

    moves = other_moves(dom_count)
    count = len(moves)
    any_space = pl.BlockSpec(memory_space=pl.ANY)
    tables, measured = pl.pallas_call(
        functools.partial(margin_kernel, dims, dom_count),
        out_shape=(
            jax.ShapeDtypeStruct((count + 1, band_pad, 3 * LANES), BF16),
            jax.ShapeDtypeStruct((3 * band_pad, entry_lanes), F32),
        ),
        in_specs=[vmem(), vmem(), smem(), vmem(), vmem(), vmem()],
        out_specs=(vmem(), vmem()),
        scratch_shapes=[
            pltpu.VMEM(((plane_count + 4) * (width_y + 4), band_pad, width_z), BF16),
            pltpu.VMEM((entry_count * proj_count, tile_len), BF16),
            pltpu.VMEM((group, 2 * band_pad, tile_len), BF16),
            pltpu.VMEM((band_pad, entry_lanes), F32),
            pltpu.VMEM((band_pad, 3 * LANES), BF16),
            pltpu.VMEM((count, band_pad, 3 * LANES), BF16),
            pltpu.SemaphoreType.DMA((count,)),
            pltpu.SemaphoreType.DMA((count,)),
        ],
        compiler_params=pltpu.CompilerParams(
            vmem_limit_bytes=VMEM_LIMIT, collective_id=1, has_side_effects=True
        ),
        cost_estimate=SMALL,
        name="margins",
    )(wavefunctions, flat, tile_rows, swap, sort, first_z)

    places = {u: 0 if u % dom_count == 0 else moves.index(u % dom_count) + 1 for u in range(-2, 3)}
    inner, edge, coef = pl.pallas_call(
        functools.partial(apply_kernel, dims, places),
        out_shape=(
            jax.ShapeDtypeStruct(wavefunctions.shape, BF16),
            jax.ShapeDtypeStruct((band_count, 4, width_y, width_z), F32),
            jax.ShapeDtypeStruct((band_pad, entry_lanes), F32),
        ),
        in_specs=[vmem(), vmem(), vmem(), vmem(), smem()] + [vmem()] * 5,
        out_specs=(any_space, any_space, vmem()),
        scratch_shapes=[
            pltpu.VMEM((row_count, band_pad, width_z), F32),
            pltpu.VMEM(wavefunctions.shape, BF16),
            pltpu.VMEM((plane_count, width_y, width_z), BF16),
            pltpu.VMEM((band_count, plane_count - 4, width_y, width_z), BF16),
            pltpu.VMEM((band_count, 4, width_y, width_z), F32),
            pltpu.SemaphoreType.DMA((band_count,)),
            pltpu.SemaphoreType.DMA((band_count,)),
        ],
        compiler_params=params,
        cost_estimate=SMALL,
        name="apply",
    )(
        tables, wavefunctions, potential, flat, tile_rows, back, sort_back, mix, second_y,
        second_z,
    )

    slots = 3 * band_devices
    forces = pl.pallas_call(
        functools.partial(force_kernel, dims, dom_count, band_devices),
        out_shape=jax.ShapeDtypeStruct((8, LANES), F32),
        in_specs=[vmem(), vmem(), vmem(), smem()] + [vmem()] * 5,
        out_specs=vmem(),
        scratch_shapes=[
            pltpu.VMEM((row_count, band_pad, width_z), BF16),
            pltpu.VMEM((group, band_pad, tile_len), BF16),
            pltpu.VMEM((band_pad, entry_lanes), F32),
            pltpu.VMEM((3, 8, LANES), F32),
            pltpu.VMEM((slots, 8, LANES), F32),
            pltpu.SemaphoreType.DMA((slots,)),
            pltpu.SemaphoreType.DMA((slots,)),
        ],
        compiler_params=pltpu.CompilerParams(
            vmem_limit_bytes=VMEM_LIMIT, collective_id=0, has_side_effects=True
        ),
        cost_estimate=SMALL,
        name="force_sum",
    )(before, after, flat, tile_rows, swap, measured, coef, weights, pick)[:3, :ATOM_DEV]

    chunk = max(band_count // 4, 1)
    applied = pl.pallas_call(
        edge_kernel,
        grid=(band_count // chunk, 2),
        out_shape=jax.ShapeDtypeStruct(wavefunctions.shape, BF16),
        in_specs=[
            pl.BlockSpec((chunk, 2, width_y, width_z), lambda i, side: (i, side, 0, 0)),
            pl.BlockSpec((chunk, 2, width_y, width_z), lambda i, side: (i, 0, 0, 0)),
            pl.BlockSpec((chunk, 2, width_y, width_z), lambda i, side: (i, 0, 0, 0)),
            pl.BlockSpec(memory_space=pl.ANY),
        ],
        out_specs=pl.BlockSpec(
            (chunk, 2, width_y, width_z),
            lambda i, side: (i, side * (plane_count // 2 - 1), 0, 0),
        ),
        input_output_aliases={3: 0},
        compiler_params=params,
        cost_estimate=SMALL,
        name="edges",
    )(edge, before, after, inner)
    return (applied, forces)


def other_moves(dom_count):
    return sorted({u % dom_count for u in range(-2, 3)} - {0})


def solution(mesh):
    placed = (
        P("band", "dom", None, None),
        P("dom", None, None),
        P("dom", None, None),
        P("dom"),
        P("dom"),
        P(),
        P("band"),
    )
    return jax.shard_map(
        per_device,
        mesh=mesh,
        in_specs=placed,
        out_specs=(P("band", "dom", None, None), P(None, "dom")),
        check_vma=False,
    )
```

time: 76.6 us -> 67.6 us (0.88)
  Pallas kernels: 56.4 us -> 52.2 us
  starting transfers between devices: 5.53 us -> 2.71 us
  local copies, waits for them, and re-layouts: 10.5 us -> 9.16 us
    pallas_call x5 -> x3, Pallas kernels: 49.8 us -> 45.7 us  [the longest x1 19.7 us: per_device(): pl.pallas_call(functools.partial(margin_kernel, dims, dom_count), out_sha...]
    ppermute x3 -> x0, starting transfers between devices: 3.79 us -> none  [per_device(): tables.append(lax.ppermute(table, 'dom', pairs))]
    unnamed x33 -> x27, local copies, waits for them, and re-layouts: 5.56 us -> 2.67 us
    slice x1, local copies, waits for them, and re-layouts: 1.59 us -> 3.26 us  [per_device(): after = lax.ppermute(wavefunctions[:, :2], 'dom', down)]
    ppermute x1, starting transfers between devices: 1.74 us -> 2.61 us  [per_device(): before = lax.ppermute(wavefunctions[:, plane_count - 2:], 'dom', up)]
  transfers between devices with their start and end apart: 5 -> 2, of which waited for: 0 -> 0; matrix products, arithmetic and copies ran while one was open for 6% -> 7% of each run, Pallas kernels for 36% -> 48%
where the time goes in v1:
time: 67.6 us; the launch traced here: 67.1 us
  Pallas kernels  52.2 us (77%)
  local copies, waits for them, and re-layouts  9.16 us (14%)
  starting transfers between devices  2.71 us (4%)
  other arithmetic  2.14 us (3%)
  between operations  0.86 us (1%)
    pallas_call x1, Pallas kernels, per_device(): pl.pallas_call(functools.partial(margin_kernel, dims, dom_count), out_sha...  19.7 us
    pallas_call x1, Pallas kernels, per_device(): pl.pallas_call(functools.partial(force_kernel, dims, dom_count, band_devi...  13.3 us
    pallas_call x1, Pallas kernels, per_device(): pl.pallas_call(functools.partial(apply_kernel, dims, places), out_shape=(...  12.7 us
    pallas_call x1, Pallas kernels, per_device(): pl.pallas_call(edge_kernel, grid=(band_count // chunk, 2), out_shape=jax....  6.57 us
    slice x1, local copies, waits for them, and re-layouts, per_device(): after = lax.ppermute(wavefunctions[:, :2], 'dom', down)  3.26 us
    unnamed x27, local copies, waits for them, and re-layouts  2.67 us
    ppermute x1, starting transfers between devices, per_device(): before = lax.ppermute(wavefunctions[:, plane_count - 2:], 'dom', up)  2.61 us
    mul x1, local copies, waits for them, and re-layouts, per_device(): mix = jnp.kron(jnp.eye(LANES // proj_count, dtype=F32), symmetric)  1.65 us
  transfers between devices with their start and end apart: 2, of which 0 were waited for; matrix products, arithmetic and copies ran while one was open for 7% of the time, Pallas kernels for 48%

profile of v1, /device:TPU:1, one launch (start us, length us, event | category | flops | bytes accessed | tf_op | source)
XLA Modules:
  0.0 67.1 jit_solution(15830767794133232598)
XLA Ops:
  0.6 0.0 copy-start.3
  0.6 0.0 copy-start.7
  0.7 0.0 copy-start.12
  0.7 0.0 copy-start.11
  0.7 0.0 copy-start.10
  0.7 0.0 copy-start.8
  0.7 0.0 copy-start
  0.7 3.3 %fusion.13 = (bf16[16,2,128,128]{3,2,1,0:T(8,128)(2,1)}, bf16[16,2,128,128]{3,2,1,0:T(8,128)(2,1)}) fusion(bf16[16,8,128,128]{3,2,1,0:T(8,128)(2,1)} %wave_ref.3), kind=kLoop, calls=%fused_computation.26 | loop fusion | bytes 4194304 | tf_op jit(solution)/shard_map/slice | solution.py:453
  4.0 0.0 copy-start.4
  4.0 0.0 copy-start.5
  4.0 0.0 copy-start.6
  4.0 0.1 collective-permute-start.1
  4.1 2.6 %collective-permute-start = (bf16[16,2,128,128]{3,2,1,0:T(8,128)(2,1)}, bf16[16,2,128,128]{3,2,1,0:T(8,128)(2,1)S(1)}, u32[]{:S(2)}, u32[]{:S(2)}) collective-permute-start(bf16[16,2,128,128]{3,2,1,0:T(8,128)(2,1)} %get-tuple-element.15), channel_id=1, source_target_pairs={{0,8},{8,16},{16,24},{24,0},{1,9},{9,17},{17,25},{25,1},{2,10},{10... | collective-permute-start | bytes 3145736 | tf_op jit(solution)/shard_map/ppermute | solution.py:452
  6.7 0.0 copy-done.12
  6.7 0.0 copy-done.11
  6.8 0.0 copy-done.10
  6.8 0.1 copy.17
  6.8 0.1 copy.18.weight_ref
  6.9 0.1 broadcast_in_dim.16
  7.0 0.7 %reshape.54 = s32[384]{0:T(512)} reshape(s32[48,8]{1,0:T(8,128)S(1)} %broadcast_in_dim.16) | data formatting | bytes 3072 | tf_op jit(solution)/shard_map/reshape | solution.py:478
  7.7 0.1 broadcast_in_dim.18
  7.7 0.1 eq.60
  7.9 1.1 %broadcast_multiply_fusion = f32[16,8,16,8]{3,2,1,0:T(8,128)} fusion(f32[8,8]{1,0:T(8,128)S(1)} %fusion.4, f32[16,16]{1,0:T(8,128)S(1)} %fusion.3), kind=kLoop, calls=%fused_computation.6 | loop fusion | flops 16384 | bytes 66816 | tf_op jit(solution)/shard_map/jit(kron)/mul | solution.py:483
  9.0 1.6 %mul.51.mix_ref = f32[128,128]{1,0:T(8,128)S(1)} reshape(f32[16,8,16,8]{3,2,1,0:T(8,128)} %broadcast_multiply_fusion) | data formatting | bytes 131072 | tf_op jit(solution)/shard_map/jit(kron)/mul | solution.py:483
  10.6 0.7 %fusion.5 = s32[384]{0:T(512)S(1)} fusion(s32[384]{0:T(512)} %reshape.54), kind=kLoop, calls=%fused_computation.14 | loop fusion | flops 2688 | bytes 3072 | tf_op jit(solution)/shard_map/add | solution.py:478
  11.3 0.2 fusion.1
  11.5 0.0 copy-done.3
  11.5 0.0 copy-done.7
  11.5 0.0 copy-done.8
  11.5 0.0 copy-done
  11.5 19.7 %margins.1 = (bf16[4,16,384]{2,1,0:T(8,128)(2,1)S(1)}, f32[48,384]{1,0:T(8,128)S(1)}) custom-call(bf16[16,8,128,128]{3,2,1,0:T(8,128)(2,1)} %wave_ref.3, bf16[288,1024]{1,0:T(8,128)(2,1)S(1)} %bitcast.9, s32[36]{0:T(128)S(1)} %copy-done.8, bf16[256,256]{1,0:T(8,128)(2,1)S(1)} %copy-done.3, bf16[384,384]{1,0:T(8,128)(2,1)S(1)} %get-tuple-element.17.sort_ref, ...), custom_call_target="tpu_custom_call" | custom-call | flops 1048576 | bytes 4096 | tf_op jit(solution)/shard_map/margins/pallas_call | solution.py:491
  31.2 0.0 copy-done.4
  31.2 0.0 copy-done.5
  31.2 0.0 copy-done.6
  31.2 12.7 %apply.1 = (bf16[16,8,128,128]{3,2,1,0:T(8,128)(2,1)}, f32[16,4,128,128]{3,2,1,0:T(8,128)}, f32[16,384]{1,0:T(8,128)S(1)}) custom-call(bf16[4,16,384]{2,1,0:T(8,128)(2,1)S(1)} %get-tuple-element.7.tables_ref, bf16[16,8,128,128]{3,2,1,0:T(8,128)(2,1)} %wave_ref.3, f32[8,128,128]{2,1,0:T(8,128)S(1)} %copy-done.4, bf16[288,1024]{1,0:T(8,128)(2,1)S(1)} %bitcast.10, ...), custom_call_target="tpu_custom_call" | custom-call | flops 1048576 | bytes 4096 | tf_op jit(solution)/shard_map/apply/pallas_call | solution.py:517
  43.9 0.1 fusion.2.pick_ref
  44.0 0.0 collective-permute-done.1.after_ref
  44.1 0.0 copy-start.9
  44.1 0.0 collective-permute-done.before_ref
  44.1 0.0 copy-start.1
  44.1 0.9 %copy-done.9 = bf16[16,2,128,128]{3,2,1,0:T(8,128)(2,1)} copy-done((bf16[16,2,128,128]{3,2,1,0:T(8,128)(2,1)}, bf16[16,2,128,128]{3,2,1,0:T(8,128)(2,1)S(1)}, u32[]{:S(2)}) %copy-start.9) | copy-done | bytes 1048600
  45.0 0.4 copy-done.1
  45.4 13.3 %force_sum.1 = f32[8,128]{1,0:T(8,128)S(1)} custom-call(bf16[16,2,128,128]{3,2,1,0:T(8,128)(2,1)} %copy-done.1, bf16[16,2,128,128]{3,2,1,0:T(8,128)(2,1)} %copy-done.9, bf16[288,1024]{1,0:T(8,128)(2,1)S(1)} %bitcast.11, s32[36]{0:T(128)S(1)} %copy-done.8, bf16[256,256]{1,0:T(8,128)(2,1)S(1)} %copy-done.3, f32[48,384]{1,0:T(8,128)S(1)} %get-tuple-element.10.meas_ref, ...), custom_call_target="tpu_custom_call" | custom-call | flops 1048576 | bytes 4096 | tf_op jit(solution)/shard_map/force_sum/pallas_call | solution.py:544
  58.7 0.6 slice.11
  59.3 0.0 copy-start.2
  59.3 1.2 %copy-done.2 = bf16[16,2,128,128]{3,2,1,0:T(8,128)(2,1)S(1)} copy-done((bf16[16,2,128,128]{3,2,1,0:T(8,128)(2,1)S(1)}, bf16[16,2,128,128]{3,2,1,0:T(8,128)(2,1)}, u32[]{:S(2)}) %copy-start.2) | copy-done | bytes 1048600
  60.5 6.6 %edges.1 = bf16[16,8,128,128]{3,2,1,0:T(8,128)(2,1)} custom-call(f32[16,4,128,128]{3,2,1,0:T(8,128)} %get-tuple-element.8.edge_ref, bf16[16,2,128,128]{3,2,1,0:T(8,128)(2,1)S(1)} %copy-done.2, bf16[16,2,128,128]{3,2,1,0:T(8,128)(2,1)} %copy-done.9, bf16[16,8,128,128]{3,2,1,0:T(8,128)(2,1)} %get-tuple-element.9.inner_ref), custom_call_target="tpu_custom_call", output_to_operand_aliasing={{}: (3, {})} | custom-call | flops 1048576 | bytes 4096 | tf_op jit(solution)/shard_map/edges/pallas_call | solution.py:566
  (7 shorter events, 0.1 us)
Async XLA Ops:
  0.6 10.8 %copy-start.3 = (bf16[256,256]{1,0:T(8,128)(2,1)S(1)}, bf16[256,256]{1,0:T(8,128)(2,1)}, u32[]{:S(2)}) copy-start(bf16[256,256]{1,0:T(8,128)(2,1)} %constant.71.clone.swap_ref.back_ref) | copy-start | bytes 393220
  0.6 10.8 %copy-start.7 = (bf16[128,128]{1,0:T(8,128)(2,1)S(1)}, bf16[128,128]{1,0:T(8,128)(2,1)}, u32[]{:S(2)}) copy-start(bf16[128,128]{1,0:T(8,128)(2,1)} %constant.72.clone.first_ref) | copy-start | bytes 98308
  0.7 6.0 %copy-start.12 = (f32[16]{0:T(128)S(1)}, f32[16]{0:T(128)}, u32[]{:S(2)}) copy-start(f32[16]{0:T(128)} %param.18) | copy-start | bytes 196
  0.7 6.0 %copy-start.11 = (s32[36]{0:T(128)S(1)}, s32[36]{0:T(128)}, u32[]{:S(2)}) copy-start(s32[36]{0:T(128)} %param.15) | copy-start | bytes 436
  0.7 6.1 %copy-start.10 = (f32[8,8]{1,0:T(8,128)S(1)}, f32[8,8]{1,0:T(8,128)}, u32[]{:S(2)}) copy-start(f32[8,8]{1,0:T(8,128)} %param.17) | copy-start | bytes 772
  0.7 10.8 %copy-start.8 = (s32[36]{0:T(128)S(1)}, s32[36]{0:T(128)}, u32[]{:S(2)}) copy-start(s32[36]{0:T(128)} %rows_ref.5) | copy-start | bytes 436
  0.7 10.8 %copy-start = (bf16[36,8,1024]{2,1,0:T(8,128)(2,1)S(1)}, bf16[36,8,1024]{2,1,0:T(8,128)(2,1)}, u32[]{:S(2)}) copy-start(bf16[36,8,1024]{2,1,0:T(8,128)(2,1)} %param.14) | copy-start | bytes 1769476
  4.0 27.2 %copy-start.4 = (f32[8,128,128]{2,1,0:T(8,128)S(1)}, f32[8,128,128]{2,1,0:T(8,128)}, u32[]{:S(2)}) copy-start(f32[8,128,128]{2,1,0:T(8,128)} %pot_ref.1) | copy-start | bytes 1572868
  4.0 27.2 %copy-start.5 = (bf16[128,256]{1,0:T(8,128)(2,1)S(1)}, bf16[128,256]{1,0:T(8,128)(2,1)}, u32[]{:S(2)}) copy-start(bf16[128,256]{1,0:T(8,128)(2,1)} %constant.74.clone.second_y_ref) | copy-start | bytes 196612
  4.0 27.2 %copy-start.6 = (bf16[128,128]{1,0:T(8,128)(2,1)S(1)}, bf16[128,128]{1,0:T(8,128)(2,1)}, u32[]{:S(2)}) copy-start(bf16[128,128]{1,0:T(8,128)(2,1)} %constant.73.clone.second_z_ref) | copy-start | bytes 98308
  4.0 40.1 %collective-permute-start.1 = (bf16[16,2,128,128]{3,2,1,0:T(8,128)(2,1)}, bf16[16,2,128,128]{3,2,1,0:T(8,128)(2,1)S(1)}, u32[]{:S(2)}, u32[]{:S(2)}) collective-permute-start(bf16[16,2,128,128]{3,2,1,0:T(8,128)(2,1)} %get-tuple-element.14), channel_id=1, source_target_pairs={{8,0},{16,8},{24,16},{0,24},{9,1},{17,9},{25,17},{1,25},{10,2},{18... | collective-permute-start | bytes 3145736 | tf_op jit(solution)/shard_map/ppermute | solution.py:453
  4.1 40.0 %collective-permute-start = (bf16[16,2,128,128]{3,2,1,0:T(8,128)(2,1)}, bf16[16,2,128,128]{3,2,1,0:T(8,128)(2,1)S(1)}, u32[]{:S(2)}, u32[]{:S(2)}) collective-permute-start(bf16[16,2,128,128]{3,2,1,0:T(8,128)(2,1)} %get-tuple-element.15), channel_id=1, source_target_pairs={{0,8},{8,16},{16,24},{24,0},{1,9},{9,17},{17,25},{25,1},{2,10},{10... | collective-permute-start | bytes 3145736 | tf_op jit(solution)/shard_map/ppermute | solution.py:452
  44.1 1.0 %copy-start.9 = (bf16[16,2,128,128]{3,2,1,0:T(8,128)(2,1)}, bf16[16,2,128,128]{3,2,1,0:T(8,128)(2,1)S(1)}, u32[]{:S(2)}) copy-start(bf16[16,2,128,128]{3,2,1,0:T(8,128)(2,1)S(1)} %collective-permute-done.1.after_ref) | copy-start | bytes 3145732
  44.1 1.3 %copy-start.1 = (bf16[16,2,128,128]{3,2,1,0:T(8,128)(2,1)}, bf16[16,2,128,128]{3,2,1,0:T(8,128)(2,1)S(1)}, u32[]{:S(2)}) copy-start(bf16[16,2,128,128]{3,2,1,0:T(8,128)(2,1)S(1)} %collective-permute-done.before_ref) | copy-start | bytes 3145732
  59.3 1.2 %copy-start.2 = (bf16[16,2,128,128]{3,2,1,0:T(8,128)(2,1)S(1)}, bf16[16,2,128,128]{3,2,1,0:T(8,128)(2,1)}, u32[]{:S(2)}) copy-start(bf16[16,2,128,128]{3,2,1,0:T(8,128)(2,1)} %copy-done.1) | copy-start | bytes 3145732

commit v2 on v1

v2 whole, which is shorter than its diff:
```python
import functools

import jax
import jax.numpy as jnp
import numpy as np
from jax import lax
from jax.experimental import pallas as pl
from jax.experimental.pallas import tpu as pltpu
from jax.sharding import PartitionSpec as P

ATOM_DEV = 12
LANES = 128
ROWS = 16
VMEM_LIMIT = 52 * 1024 * 1024
F32 = jnp.float32
BF16 = jnp.bfloat16
HIGHEST = lax.Precision.HIGHEST


def vmem():
    return pl.BlockSpec(memory_space=pltpu.VMEM)


def smem():
    return pl.BlockSpec(memory_space=pltpu.SMEM)


def dot(a, b):
    return jnp.dot(a, b, preferred_element_type=F32)


def dot_nt(a, b, precision=None):
    return lax.dot_general(
        a, b, (((1,), (1,)), ((), ())), precision=precision, preferred_element_type=F32
    )


def circulant(width, taps):
    table = np.zeros((width, width), np.float32)
    for offset, value in taps.items():
        for target in range(width):
            table[(target + offset) % width, target] += value
    return table


def band_swap(band_count, band_pad):
    table = np.zeros((ROWS * band_pad, band_count * ROWS), np.float32)
    for y in range(ROWS):
        for b in range(band_count):
            table[y * band_pad + b, b * ROWS + y] = 1.0
    return table


def pick_groups(whole, count, height, proj_count):
    width = count * proj_count
    whole = whole.reshape(count, height, width)
    lane = lax.broadcasted_iota(jnp.int32, (count, height, width), 2) // proj_count
    item = lax.broadcasted_iota(jnp.int32, (count, height, width), 0)
    return jnp.sum(jnp.where(lane == item, whole, 0.0), axis=0)


def turn_pair(swap, left, right):
    return dot(swap, jnp.concatenate([left, right], axis=1)).astype(BF16)


def signal_all(devices):
    barrier = pltpu.get_barrier_semaphore()
    for device in devices:
        pl.semaphore_signal(
            barrier, inc=1, device_id=device, device_id_type=pl.DeviceIdType.MESH
        )


def wait_all(devices):
    pl.semaphore_wait(pltpu.get_barrier_semaphore(), len(devices))


def iota(shape, axis):
    return lax.broadcasted_iota(jnp.int32, shape, axis)


def remote(src, dst, send, recv, device):
    return pltpu.make_async_remote_copy(
        src_ref=src, dst_ref=dst, send_sem=send, recv_sem=recv, device_id=device,
        device_id_type=pl.DeviceIdType.MESH,
    )


def whole_kernel(
    dims, dom_count, band_devices, places, wave_hbm, pot_ref, proj_ref, atoms_ref, rows_ref,
    row_ref, coupling_ref, weight_ref, swap_ref, first_ref, second_y_ref, second_z_ref,
    out_ref, force_ref, wave_ref, halo_ref, turned_ref, proj_z_ref, lhs_ref, margin_ref, meas_ref,
    sort_ref, pick_ref, hit_ref, own_ref, table_ref, term_ref, part_ref, scale_ref, edge_ref,
    field_ref, extra_ref, sums_ref, held_ref, load_sem, halo_send, halo_recv, table_send,
    table_recv, force_send, force_recv,
):
    band_count, band_pad, plane_count, width_y, entry_count, proj_count, depth = dims
    stride = width_y + 4
    row_count = plane_count * width_y
    group = LANES // proj_count
    lanes = meas_ref.shape[1]
    own = lax.axis_index("dom")
    band = lax.axis_index("band")
    moves = other_moves(dom_count)
    partners = [
        (s, t) for t in range(band_devices) for s in (-1, 0, 1) if (s, t) != (0, 0)
    ]

    def device(s, t):
        return {
            "dom": lax.rem(own + s + dom_count, dom_count),
            "band": lax.rem(band + t, band_devices),
        }

    greeted = sorted({(s % dom_count, t) for s, t in partners} | {(u, 0) for u in moves})
    signal_all([device(s, t) for s, t in greeted])
    load = pltpu.make_async_copy(wave_hbm, wave_ref, load_sem)
    load.start()

    turned_ref[: 2 * stride] = jnp.zeros((2 * stride, band_pad, LANES), BF16)
    turned_ref[(plane_count + 2) * stride :] = jnp.zeros((2 * stride, band_pad, LANES), BF16)
    inner = (plane_count - 4) * width_y
    wait_all(greeted)

    halos = [
        remote(
            wave_hbm.at[:, pl.ds(plane_count - 2, 2)], halo_ref.at[0], halo_send.at[0],
            halo_recv.at[0], device(1, 0),
        ),
        remote(
            wave_hbm.at[:, pl.ds(0, 2)], halo_ref.at[1], halo_send.at[1], halo_recv.at[1],
            device(-1, 0),
        ),
    ]
    for copy in halos:
        copy.start()

    field_ref[2 * width_y : 2 * width_y + inner] = jnp.zeros((inner, band_pad, LANES), BF16)
    atoms = atoms_ref[...]
    owner = jnp.zeros_like(atoms)
    for k in range(1, dom_count):
        owner = owner + (atoms >= k * ATOM_DEV).astype(jnp.int32)
    within = atoms - owner * ATOM_DEV
    relative = owner - own + 1
    relative = jnp.where(relative < 0, relative + dom_count, relative)
    relative = jnp.where(relative >= dom_count, relative - dom_count, relative)
    target = iota((entry_count, 3 * LANES), 1)
    first_lane = relative * LANES + within * proj_count
    shift = target - first_lane
    near = ((shift >= 0) & (shift < proj_count)).astype(F32).astype(BF16)
    chosen = (target == relative * LANES + within).astype(F32).astype(BF16)
    entry_of = (iota((lanes, entry_count), 0) // proj_count == iota((lanes, entry_count), 1))
    entry_of = entry_of.astype(F32).astype(BF16)
    square = (lanes, 3 * LANES)
    same = iota(square, 0) % proj_count == iota(square, 1) % proj_count
    sort_ref[...] = jnp.where(same, dot(entry_of, near), 0.0).astype(BF16)
    pick_ref[...] = dot(entry_of, chosen).astype(BF16)
    spots = row_ref.shape[1]
    column = iota((spots, depth * spots), 1)
    entry = (column // LANES) * group + column % group
    entry_at = (entry == iota((spots, depth * spots), 0)).astype(F32)
    goal = jnp.dot(
        jnp.broadcast_to(row_ref[...], (8, spots)), entry_at, precision=HIGHEST,
        preferred_element_type=F32,
    )[:1]
    goal = goal + ((iota(goal.shape, 1) % LANES) // group).astype(F32)
    for x in range(plane_count):
        grid_row = (iota((width_y, depth * spots), 0) + x * width_y).astype(F32)
        hit_ref[x * width_y : (x + 1) * width_y] = (grid_row == goal).astype(F32).astype(BF16)
    scale_ref[...] = (pot_ref[...] * -24.0).astype(BF16)
    for j in range(depth):
        columns = slice(j * LANES, (j + 1) * LANES)
        proj_z_ref[:, columns] = (
            dot(proj_ref[:, columns], first_ref[...]) * (-1.0 / 12.0)
        ).astype(BF16)
    meas_ref[...] = jnp.zeros_like(meas_ref)
    margin_ref[...] = jnp.zeros_like(margin_ref)
    extra_ref[...] = jnp.zeros_like(extra_ref)
    load.wait()

    def turn(step, carry):
        rows = pl.ds(pl.multiple_of(step * ROWS, ROWS), ROWS)
        for x in range(0, plane_count, 2):
            moved = turn_pair(
                swap_ref[...],
                wave_ref[:, x, rows, :].reshape(band_count * ROWS, LANES),
                wave_ref[:, x + 1, rows, :].reshape(band_count * ROWS, LANES),
            )
            for k in range(2):
                turned_ref[pl.ds((x + k + 2) * stride + 2 + step * ROWS, ROWS)] = moved[
                    :, k * LANES : (k + 1) * LANES
                ].reshape(ROWS, band_pad, LANES)
        return carry

    lax.fori_loop(0, width_y // ROWS, turn, 0)
    for x in range(2, plane_count + 2):
        base = x * stride
        turned_ref[base : base + 2] = turned_ref[base + width_y : base + width_y + 2]
        turned_ref[base + width_y + 2 : base + width_y + 4] = turned_ref[base + 2 : base + 4]

    bits = width_y.bit_length() - 1

    def place(row, j):
        at = row + j
        return at + 4 * lax.shift_right_logical(at, bits) + 2 * stride + 2

    def each_group(body, height, weight_list):
        for start in range(0, entry_count, group):
            count = min(group, entry_count - start)
            width = count * proj_count
            first = start * proj_count
            lax.fori_loop(0, count, functools.partial(body, start), 0, unroll=4)
            lhs = lhs_ref[:count, :height].reshape(count * height, depth * LANES)
            for weight_ref_, result_ref, low in weight_list:
                whole = dot_nt(lhs, weight_ref_[first : first + width])
                result_ref[low : low + height, first : first + width] = pick_groups(
                    whole, count, height, proj_count
                )

    def fetch(start, k, carry):
        row = rows_ref[start + k]
        for j in range(depth):
            lhs_ref[k, :band_pad, j * LANES : (j + 1) * LANES] = turned_ref[place(row, j)]
        return carry

    each_group(fetch, band_pad, [(proj_ref, margin_ref, 0), (proj_z_ref, meas_ref, 2 * band_pad)])
    own_ref[...] = dot(margin_ref[...].astype(BF16), sort_ref[...]).astype(BF16)
    copies = []
    for slot, u in enumerate(moves):
        copy = remote(
            own_ref, table_ref.at[slot], table_send.at[slot], table_recv.at[slot], device(-u, 0)
        )
        copy.start()
        copies.append(copy)

    def derive(start, k, carry):
        row = rows_ref[start + k]
        for j in range(depth):
            at = place(row, j)
            columns = slice(j * LANES, (j + 1) * LANES)
            for part, step in ((0, stride), (1, 1)):
                far = turned_ref[at - 2 * step].astype(F32) - turned_ref[at + 2 * step].astype(F32)
                side = turned_ref[at + step].astype(F32) - turned_ref[at - step].astype(F32)
                lhs_ref[k, part * band_pad : (part + 1) * band_pad, columns] = (
                    far * (1.0 / 12.0) + side * (2.0 / 3.0)
                ).astype(BF16)
        return carry

    each_group(derive, 2 * band_pad, [(proj_ref, meas_ref, 0)])

    for copy in copies:
        copy.wait_recv()
    tables = [own_ref[...]] + [table_ref[slot] for slot in range(len(moves))]
    totals = []
    for s in (-1, 0, 1):
        total = jnp.zeros((band_pad, LANES), F32)
        for u in (s - 1, s, s + 1):
            block = s - u + 1
            total = total + tables[places[u]][:, block * LANES : (block + 1) * LANES].astype(F32)
        totals.append(total)
    inside = (iota((LANES, proj_count), 0) % proj_count == iota((LANES, proj_count), 1)).astype(F32)
    spread = jnp.dot(inside, coupling_ref[...], precision=HIGHEST, preferred_element_type=F32)
    mix = 0.5 * (dot_nt(spread, inside, HIGHEST) + dot_nt(inside, spread, HIGHEST))
    square = (LANES, LANES)
    mix = jnp.where(
        iota(square, 0) // proj_count == iota(square, 1) // proj_count, mix, 0.0
    )
    scaled = jnp.dot(
        jnp.concatenate(totals, axis=0), mix, precision=HIGHEST, preferred_element_type=F32
    )
    scaled = jnp.concatenate(
        [scaled[s * band_pad : (s + 1) * band_pad] for s in range(3)], axis=1
    )
    high = scaled.astype(BF16)
    low = (scaled - high.astype(F32)).astype(BF16)
    sorted_back = dot_nt(jnp.concatenate([high, low], axis=0), sort_ref[...])
    half = sorted_back[:band_pad]
    weighted = (half + sorted_back[band_pad:]) * weight_ref[...]

    for index, start in enumerate(range(0, entry_count, group)):
        width = min(group, entry_count - start) * proj_count
        first = start * proj_count
        shape = (band_pad, group, width)
        held = jnp.broadcast_to(half[:, first : first + width][:, None], shape)
        held = jnp.where(iota(shape, 2) // proj_count == iota(shape, 1), held, 0.0)
        held = held.reshape(band_pad * group, width).astype(BF16)
        for j in range(depth):
            terms = dot(held, proj_ref[first : first + width, j * LANES : (j + 1) * LANES])
            at = index * LANES + j * group
            term_ref[:, at : at + group, :] = (
                (terms * -24.0).astype(BF16).reshape(band_pad, group, LANES)
            )

    def each_pair(pair, carry):
        terms = jnp.concatenate([term_ref[pair * 2], term_ref[pair * 2 + 1]], axis=1)
        part_ref[...] = dot(hit_ref[...], terms).astype(BF16)
        for x in range(plane_count):
            tops, adds = [], []
            for k in range(2):
                b = pair * 2 + k

                def near(offset):
                    return [
                        wave_ref[b, x + o]
                        for o in (offset, -offset)
                        if 0 <= x + o < plane_count
                    ]

                here = wave_ref[b, x]
                one, two = near(1), near(2)
                side = sum(one[1:], one[0]) * jnp.asarray(16.0, BF16)
                side = side - sum(two[1:], two[0])
                part = part_ref[x * width_y : (x + 1) * width_y, k * LANES : (k + 1) * LANES]
                adds.append(side + (scale_ref[x] * here + part))
                tops.append(here)
            both = jnp.concatenate(
                [jnp.concatenate(tops, axis=1), jnp.concatenate(adds, axis=1)], axis=0
            )
            lap = dot(second_y_ref[...], both)
            along_z = dot(jnp.concatenate(tops, axis=0), second_z_ref[...])
            for k in range(2):
                b = pair * 2 + k
                total = lap[:, k * LANES : (k + 1) * LANES]
                total = total + along_z[k * width_y : (k + 1) * width_y]
                total = total * (-1.0 / 24.0)
                if x < 2:
                    edge_ref[b, x] = total
                elif x >= plane_count - 2:
                    edge_ref[b, x - plane_count + 4] = total
                else:
                    out_ref[b, x] = total.astype(BF16)
        return carry

    lax.fori_loop(0, band_count // 2, each_pair, 0)

    for copy in halos:
        copy.wait_recv()

    def halo_rows(step, carry):
        rows = pl.ds(pl.multiple_of(step * ROWS, ROWS), ROWS)
        b2 = halo_ref[0, :, 0, rows, :].astype(F32)
        b1 = halo_ref[0, :, 1, rows, :].astype(F32)
        a1 = halo_ref[1, :, 0, rows, :].astype(F32)
        a2 = halo_ref[1, :, 1, rows, :].astype(F32)
        last = plane_count - 1
        for x, left, right in ((0, b2 - 8.0 * b1, b1), (last - 1, -a1, 8.0 * a1 - a2)):
            moved = turn_pair(
                swap_ref[...],
                *[
                    (value * (1.0 / 12.0)).astype(BF16).reshape(band_count * ROWS, LANES)
                    for value in (left, right)
                ],
            )
            for k in range(2):
                field_ref[pl.ds((x + k) * width_y + step * ROWS, ROWS)] = moved[
                    :, k * LANES : (k + 1) * LANES
                ].reshape(ROWS, band_pad, LANES)
        return carry

    lax.fori_loop(0, width_y // ROWS, halo_rows, 0)

    def fetch_halo(start, k, carry):
        tile = field_ref[pl.ds(rows_ref[start + k], depth)]
        for j in range(depth):
            lhs_ref[k, :band_pad, j * LANES : (j + 1) * LANES] = tile[j]
        return carry

    each_group(fetch_halo, band_pad, [(proj_ref, extra_ref, 0)])
    sums = []
    for k in range(3):
        held = meas_ref[k * band_pad : (k + 1) * band_pad]
        if k == 0:
            held = held + extra_ref[...]
        sums.append(jnp.sum(weighted * held, axis=0, keepdims=True))
    sums = jnp.concatenate(sums + [jnp.zeros((5, lanes), F32)], axis=0)
    high = sums.astype(BF16)
    rest = sums - high.astype(F32)
    middle = rest.astype(BF16)
    low = (rest - middle.astype(F32)).astype(BF16)
    pieces = jnp.concatenate([high, middle, low, jnp.zeros_like(low)], axis=0)
    spread = dot(pieces, pick_ref[...])
    spread = spread[:8] + spread[8:16] + spread[16:24]
    for s in range(3):
        sums_ref[s] = spread[:, s * LANES : (s + 1) * LANES]
    force_copies = []
    for s, t in partners:
        slot = (s + 1) * band_devices + t
        copy = remote(
            sums_ref.at[s + 1], held_ref.at[slot], force_send.at[slot], force_recv.at[slot],
            device(s, t),
        )
        copy.start()
        force_copies.append((slot, copy))

    def edges(b, carry):
        b2 = halo_ref[0, b, 0].astype(F32)
        b1 = halo_ref[0, b, 1].astype(F32)
        a1 = halo_ref[1, b, 0].astype(F32)
        a2 = halo_ref[1, b, 1].astype(F32)
        last = plane_count - 1
        share = 1.0 / 24.0
        out_ref[b, 0] = (edge_ref[b, 0] + (b2 - 16.0 * b1) * share).astype(BF16)
        out_ref[b, 1] = (edge_ref[b, 1] + b1 * share).astype(BF16)
        out_ref[b, last - 1] = (edge_ref[b, 2] + a1 * share).astype(BF16)
        out_ref[b, last] = (edge_ref[b, 3] + (a2 - 16.0 * a1) * share).astype(BF16)
        return carry

    lax.fori_loop(0, band_count, edges, 0)
    total = sums_ref[1]
    for slot, copy in force_copies:
        copy.wait_recv()
        total = total + held_ref[slot]
    force_ref[...] = total
    for copy in halos + copies + [copy for _, copy in force_copies]:
        copy.wait_send()


def per_device(
    wavefunctions, potential, projectors, margin_atoms, tile_rows, coupling, band_weights
):
    band_count, plane_count, width_y, width_z = wavefunctions.shape
    entry_count, proj_count, tile_len = projectors.shape
    depth = tile_len // width_z
    row_count = plane_count * width_y
    band_pad = max(band_count, ROWS)
    dims = (band_count, band_pad, plane_count, width_y, entry_count, proj_count, depth)
    dom_count = lax.axis_size("dom")
    band_devices = lax.axis_size("band")
    group = LANES // proj_count
    lanes = -(-entry_count * proj_count // LANES) * LANES
    spots = lanes // proj_count

    swap = jnp.asarray(band_swap(band_count, band_pad), BF16)
    first_z = jnp.asarray(circulant(width_z, {-2: 1.0, -1: -8.0, 1: 8.0, 2: -1.0}), BF16)
    second_z = jnp.asarray(
        circulant(width_z, {-2: -1.0, -1: 16.0, 0: -90.0, 1: 16.0, 2: -1.0}), BF16
    )
    second_y = circulant(width_y, {-2: -1.0, -1: 16.0, 1: 16.0, 2: -1.0})
    second_y = jnp.asarray(
        np.concatenate([second_y, np.eye(width_y, dtype=np.float32)], axis=1), BF16
    )
    weights = jnp.pad(-2.0 * band_weights, (0, band_pad - band_count))[:, None]
    flat = projectors.reshape(entry_count * proj_count, tile_len)
    row_line = jnp.pad(
        tile_rows.astype(F32), (0, spots - entry_count), constant_values=-4096.0
    )[None]

    moves = other_moves(dom_count)
    places = {u: 0 if u % dom_count == 0 else moves.index(u % dom_count) + 1 for u in range(-2, 3)}
    count = len(moves)
    slots = 3 * band_devices
    applied, forces = pl.pallas_call(
        functools.partial(whole_kernel, dims, dom_count, band_devices, places),
        out_shape=(
            jax.ShapeDtypeStruct(wavefunctions.shape, BF16),
            jax.ShapeDtypeStruct((8, LANES), F32),
        ),
        in_specs=[pl.BlockSpec(memory_space=pl.ANY), vmem(), vmem(), vmem(), smem()]
        + [vmem()] * 7,
        out_specs=(vmem(), vmem()),
        scratch_shapes=[
            pltpu.VMEM(wavefunctions.shape, BF16),
            pltpu.VMEM((2, band_count, 2, width_y, width_z), BF16),
            pltpu.VMEM(((plane_count + 4) * (width_y + 4), band_pad, width_z), BF16),
            pltpu.VMEM((entry_count * proj_count, tile_len), BF16),
            pltpu.VMEM((group, 2 * band_pad, tile_len), BF16),
            pltpu.VMEM((band_pad, lanes), F32),
            pltpu.VMEM((3 * band_pad, lanes), F32),
            pltpu.VMEM((lanes, 3 * LANES), BF16),
            pltpu.VMEM((lanes, 3 * LANES), BF16),
            pltpu.VMEM((row_count, depth * spots), BF16),
            pltpu.VMEM((band_pad, 3 * LANES), BF16),
            pltpu.VMEM((count, band_pad, 3 * LANES), BF16),
            pltpu.VMEM((band_pad, depth * spots, width_z), BF16),
            pltpu.VMEM((row_count, 2 * width_z), BF16),
            pltpu.VMEM((plane_count, width_y, width_z), BF16),
            pltpu.VMEM((band_count, 4, width_y, width_z), F32),
            pltpu.VMEM((row_count, band_pad, width_z), BF16),
            pltpu.VMEM((band_pad, lanes), F32),
            pltpu.VMEM((3, 8, LANES), F32),
            pltpu.VMEM((slots, 8, LANES), F32),
            pltpu.SemaphoreType.DMA,
            pltpu.SemaphoreType.DMA((2,)),
            pltpu.SemaphoreType.DMA((2,)),
            pltpu.SemaphoreType.DMA((count,)),
            pltpu.SemaphoreType.DMA((count,)),
            pltpu.SemaphoreType.DMA((slots,)),
            pltpu.SemaphoreType.DMA((slots,)),
        ],
        compiler_params=pltpu.CompilerParams(
            vmem_limit_bytes=VMEM_LIMIT, collective_id=0, has_side_effects=True
        ),
        cost_estimate=pl.CostEstimate(
            flops=8 << 30, bytes_accessed=10 << 20, transcendentals=0
        ),
        name="step",
    )(
        wavefunctions, potential, flat, margin_atoms[:, None], tile_rows, row_line, coupling,
        weights, swap, first_z, second_y, second_z,
    )
    return (applied, forces[:3, :ATOM_DEV])


def other_moves(dom_count):
    return sorted({u % dom_count for u in range(-2, 3)} - {0})


def solution(mesh):
    placed = (
        P("band", "dom", None, None),
        P("dom", None, None),
        P("dom", None, None),
        P("dom"),
        P("dom"),
        P(),
        P("band"),
    )
    return jax.shard_map(
        per_device,
        mesh=mesh,
        in_specs=placed,
        out_specs=(P("band", "dom", None, None), P(None, "dom")),
        check_vma=False,
    )
```

time: 67.6 us -> 68.3 us (1.010)
  local copies, waits for them, and re-layouts: 9.16 us -> 12.9 us
  starting transfers between devices: 2.71 us -> 0 us
  other arithmetic: 2.14 us -> 1.32 us
  Pallas kernels: 52.2 us -> 52.9 us
    unnamed x27 -> x17, local copies, waits for them, and re-layouts: 2.67 us -> 11.5 us
    slice x2 -> x1, local copies, waits for them, and re-layouts: 3.84 us -> 0.58 us  [per_device(): return (applied, forces[:3, :ATOM_DEV])]
    ppermute x2 -> x0, starting transfers between devices: 2.71 us -> none  [the longest x1 2.61 us: per_device(): before = lax.ppermute(wavefunctions[:, plane_count - 2:], 'dom', up)]
    mul x1 -> x0, local copies, waits for them, and re-layouts: 1.65 us -> none  [per_device(): mix = jnp.kron(jnp.eye(LANES // proj_count, dtype=F32), symmetric)]
    mul x2 -> x0, other arithmetic: 1.12 us -> none  [the longest x1 1.11 us: per_device(): mix = jnp.kron(jnp.eye(LANES // proj_count, dtype=F32), symmetric)]
    add x3 -> x0, other arithmetic: 0.72 us -> none  [the longest x1 0.68 us: per_device(): first_lane = jnp.repeat(first_lane, proj_count) + lane % proj_count]
    pallas_call x4 -> x1, Pallas kernels: 52.2 us -> 52.9 us  [per_device(): pl.pallas_call(functools.partial(whole_kernel, dims, dom_count, band_devi...]
  transfers between devices with their start and end apart: 2 -> 0, of which waited for: 0 -> 0; matrix products, arithmetic and copies ran while one was open for 7% -> 0% of each run, Pallas kernels for 48% -> 0%
where the time goes in v2:
time: 68.3 us; the launch traced here: 67.8 us
  Pallas kernels  52.9 us (77%)
  local copies, waits for them, and re-layouts  12.9 us (19%)
  other arithmetic  1.32 us (2%)
    pallas_call x1, Pallas kernels, per_device(): pl.pallas_call(functools.partial(whole_kernel, dims, dom_count, band_devi...  52.9 us
    unnamed x17, local copies, waits for them, and re-layouts  11.5 us

profile of v2, /device:TPU:1, one launch (start us, length us, event | category | flops | bytes accessed | tf_op | source)
XLA Modules:
  0.0 67.8 jit_solution(13523861299968015825)
XLA Ops:
  0.6 0.7 multiply_bitcast_fusion
  1.3 0.7 convert_element_type.3
  2.0 0.1 copy.14.weight_ref
  2.0 0.7 %copy.13.atoms_ref = s32[36,1]{1,0:T(8,128)S(1)} copy(s32[36,1]{0,1:T(1,128)} %bitcast.7) | data formatting | bytes 288 | tf_op jit(solution)/shard_map/broadcast_in_dim | solution.py:498
  2.8 0.0 copy-start
  2.8 1.1 %copy-done = bf16[36,8,1024]{2,1,0:T(8,128)(2,1)S(1)} copy-done((bf16[36,8,1024]{2,1,0:T(8,128)(2,1)S(1)}, bf16[36,8,1024]{2,1,0:T(8,128)(2,1)}, u32[]{:S(2)}) %copy-start) | copy-done | bytes 589848
  3.8 0.0 copy-start.1
  3.9 1.0 %copy-done.1 = f32[8,128,128]{2,1,0:T(8,128)S(1)} copy-done((f32[8,128,128]{2,1,0:T(8,128)S(1)}, f32[8,128,128]{2,1,0:T(8,128)}, u32[]{:S(2)}) %copy-start.1) | copy-done | bytes 524312
  4.9 0.0 copy-start.2
  4.9 0.7 %copy-done.2 = f32[8,8]{1,0:T(8,128)S(1)} copy-done((f32[8,8]{1,0:T(8,128)S(1)}, f32[8,8]{1,0:T(8,128)}, u32[]{:S(2)}) %copy-start.2) | copy-done | bytes 280
  5.6 0.0 copy-start.3
  5.6 0.7 copy-done.3
  6.2 0.0 copy-start.4
  6.2 0.9 %copy-done.4 = bf16[256,256]{1,0:T(8,128)(2,1)S(1)} copy-done((bf16[256,256]{1,0:T(8,128)(2,1)S(1)}, bf16[256,256]{1,0:T(8,128)(2,1)}, u32[]{:S(2)}) %copy-start.4) | copy-done | bytes 131096
  7.1 0.0 copy-start.5
  7.1 0.8 %copy-done.5 = bf16[128,256]{1,0:T(8,128)(2,1)S(1)} copy-done((bf16[128,256]{1,0:T(8,128)(2,1)S(1)}, bf16[128,256]{1,0:T(8,128)(2,1)}, u32[]{:S(2)}) %copy-start.5) | copy-done | bytes 65560
  8.0 0.0 copy-start.6
  8.0 0.8 %copy-done.6 = bf16[128,128]{1,0:T(8,128)(2,1)S(1)} copy-done((bf16[128,128]{1,0:T(8,128)(2,1)S(1)}, bf16[128,128]{1,0:T(8,128)(2,1)}, u32[]{:S(2)}) %copy-start.6) | copy-done | bytes 32792
  8.7 0.0 copy-start.7
  8.7 0.8 %copy-done.7 = bf16[128,128]{1,0:T(8,128)(2,1)S(1)} copy-done((bf16[128,128]{1,0:T(8,128)(2,1)S(1)}, bf16[128,128]{1,0:T(8,128)(2,1)}, u32[]{:S(2)}) %copy-start.7) | copy-done | bytes 32792
  9.5 52.9 %step.1 = (bf16[16,8,128,128]{3,2,1,0:T(8,128)(2,1)}, f32[8,128]{1,0:T(8,128)S(1)}) custom-call(bf16[16,8,128,128]{3,2,1,0:T(8,128)(2,1)} %wave_hbm.1, f32[8,128,128]{2,1,0:T(8,128)S(1)} %copy-done.1, bf16[288,1024]{1,0:T(8,128)(2,1)S(1)} %bitcast.6, s32[36,1]{1,0:T(8,128)S(1)} %copy.13.atoms_ref, s32[36]{0:T(128)S(1)} %copy-done.3, ...), custom_call_target="tpu_custom_call" | custom-call | flops 8589934592 | bytes 10485760 | tf_op jit(solution)/shard_map/step/pallas_call | solution.py:452
  62.4 0.6 slice.3
  63.0 4.8 %copy.16 = bf16[16,8,128,128]{3,2,1,0:T(8,128)(2,1)} copy(bf16[16,8,128,128]{3,2,1,0:T(8,128)(2,1)} %get-tuple-element.8) | data formatting | bytes 8388608
  (1 shorter events, 0.0 us)
Async XLA Ops:
  2.8 1.1 %copy-start = (bf16[36,8,1024]{2,1,0:T(8,128)(2,1)S(1)}, bf16[36,8,1024]{2,1,0:T(8,128)(2,1)}, u32[]{:S(2)}) copy-start(bf16[36,8,1024]{2,1,0:T(8,128)(2,1)} %param.13) | copy-start | bytes 1769476
  3.8 1.0 %copy-start.1 = (f32[8,128,128]{2,1,0:T(8,128)S(1)}, f32[8,128,128]{2,1,0:T(8,128)}, u32[]{:S(2)}) copy-start(f32[8,128,128]{2,1,0:T(8,128)} %pot_ref.1) | copy-start | bytes 1572868
  4.9 0.7 %copy-start.2 = (f32[8,8]{1,0:T(8,128)S(1)}, f32[8,8]{1,0:T(8,128)}, u32[]{:S(2)}) copy-start(f32[8,8]{1,0:T(8,128)} %coupling_ref.1) | copy-start | bytes 772
  5.6 0.7 copy-start.3
  6.2 0.9 %copy-start.4 = (bf16[256,256]{1,0:T(8,128)(2,1)S(1)}, bf16[256,256]{1,0:T(8,128)(2,1)}, u32[]{:S(2)}) copy-start(bf16[256,256]{1,0:T(8,128)(2,1)} %constant.5.clone.swap_ref) | copy-start | bytes 393220
  7.1 0.8 %copy-start.5 = (bf16[128,256]{1,0:T(8,128)(2,1)S(1)}, bf16[128,256]{1,0:T(8,128)(2,1)}, u32[]{:S(2)}) copy-start(bf16[128,256]{1,0:T(8,128)(2,1)} %constant.16.clone.second_y_ref) | copy-start | bytes 196612
  8.0 0.8 %copy-start.6 = (bf16[128,128]{1,0:T(8,128)(2,1)S(1)}, bf16[128,128]{1,0:T(8,128)(2,1)}, u32[]{:S(2)}) copy-start(bf16[128,128]{1,0:T(8,128)(2,1)} %constant.15.clone.second_z_ref) | copy-start | bytes 98308
  8.7 0.8 %copy-start.7 = (bf16[128,128]{1,0:T(8,128)(2,1)S(1)}, bf16[128,128]{1,0:T(8,128)(2,1)}, u32[]{:S(2)}) copy-start(bf16[128,128]{1,0:T(8,128)(2,1)} %constant.14.clone.first_ref) | copy-start | bytes 98308

commit v3 on v2

--- a/solution.py
+++ b/solution.py
@@ -11,7 +11,7 @@
 ATOM_DEV = 12
 LANES = 128
 ROWS = 16
-VMEM_LIMIT = 52 * 1024 * 1024
+VMEM_LIMIT = 62 * 1024 * 1024
 F32 = jnp.float32
 BF16 = jnp.bfloat16
 HIGHEST = lax.Precision.HIGHEST
@@ -88,11 +88,11 @@
 
 def whole_kernel(
     dims, dom_count, band_devices, places, wave_hbm, pot_ref, proj_ref, atoms_ref, rows_ref,
-    row_ref, coupling_ref, weight_ref, swap_ref, first_ref, second_y_ref, second_z_ref,
-    out_ref, force_ref, wave_ref, halo_ref, turned_ref, proj_z_ref, lhs_ref, margin_ref, meas_ref,
+    coupling_ref, weight_ref, swap_ref, first_ref, second_y_ref, second_z_ref,
+    out_hbm, force_ref, out_ref, wave_ref, halo_ref, turned_ref, proj_z_ref, lhs_ref, margin_ref, meas_ref,
     sort_ref, pick_ref, hit_ref, own_ref, table_ref, term_ref, part_ref, scale_ref, edge_ref,
     field_ref, extra_ref, sums_ref, held_ref, load_sem, halo_send, halo_recv, table_send,
-    table_recv, force_send, force_recv,
+    table_recv, force_send, force_recv, out_sem,
 ):
     band_count, band_pad, plane_count, width_y, entry_count, proj_count, depth = dims
     stride = width_y + 4
@@ -136,7 +136,16 @@
         copy.start()
 
     field_ref[2 * width_y : 2 * width_y + inner] = jnp.zeros((inner, band_pad, LANES), BF16)
-    atoms = atoms_ref[...]
+    spots = lanes // proj_count
+    slot_of = iota((entry_count, 3 * LANES), 0)
+    atoms = jnp.zeros((entry_count, 3 * LANES), jnp.int32)
+    line = jnp.full((8, spots), -4096, jnp.int32)
+    for e in range(entry_count):
+        atoms = jnp.where(slot_of == e, atoms_ref[e], atoms)
+        line = jnp.where(iota((8, spots), 1) == e, rows_ref[e], line)
+    weight = jnp.zeros((band_pad, lanes), F32)
+    for b in range(band_count):
+        weight = jnp.where(iota((band_pad, lanes), 0) == b, -2.0 * weight_ref[b], weight)
     owner = jnp.zeros_like(atoms)
     for k in range(1, dom_count):
         owner = owner + (atoms >= k * ATOM_DEV).astype(jnp.int32)
@@ -155,13 +164,11 @@
     same = iota(square, 0) % proj_count == iota(square, 1) % proj_count
     sort_ref[...] = jnp.where(same, dot(entry_of, near), 0.0).astype(BF16)
     pick_ref[...] = dot(entry_of, chosen).astype(BF16)
-    spots = row_ref.shape[1]
     column = iota((spots, depth * spots), 1)
     entry = (column // LANES) * group + column % group
     entry_at = (entry == iota((spots, depth * spots), 0)).astype(F32)
     goal = jnp.dot(
-        jnp.broadcast_to(row_ref[...], (8, spots)), entry_at, precision=HIGHEST,
-        preferred_element_type=F32,
+        line.astype(F32), entry_at, precision=HIGHEST, preferred_element_type=F32
     )[:1]
     goal = goal + ((iota(goal.shape, 1) % LANES) // group).astype(F32)
     for x in range(plane_count):
@@ -275,7 +282,7 @@
     low = (scaled - high.astype(F32)).astype(BF16)
     sorted_back = dot_nt(jnp.concatenate([high, low], axis=0), sort_ref[...])
     half = sorted_back[:band_pad]
-    weighted = (half + sorted_back[band_pad:]) * weight_ref[...]
+    weighted = (half + sorted_back[band_pad:]) * weight
 
     for index, start in enumerate(range(0, entry_count, group)):
         width = min(group, entry_count - start) * proj_count
@@ -290,6 +297,18 @@
             term_ref[:, at : at + group, :] = (
                 (terms * -24.0).astype(BF16).reshape(band_pad, group, LANES)
             )
+
+    def inner_copy(b):
+        planes = pl.ds(2, plane_count - 4)
+        return pltpu.make_async_copy(
+            out_ref.at[b, planes], out_hbm.at[b, planes], out_sem.at[b]
+        )
+
+    def edge_copy(side):
+        planes = pl.ds(side * (plane_count - 2), 2)
+        return pltpu.make_async_copy(
+            out_ref.at[:, planes], out_hbm.at[:, planes], out_sem.at[band_count + side]
+        )
 
     def each_pair(pair, carry):
         terms = jnp.concatenate([term_ref[pair * 2], term_ref[pair * 2 + 1]], axis=1)
@@ -329,21 +348,24 @@
                     edge_ref[b, x - plane_count + 4] = total
                 else:
                     out_ref[b, x] = total.astype(BF16)
+        for k in range(2):
+            inner_copy(pair * 2 + k).start()
         return carry
 
     lax.fori_loop(0, band_count // 2, each_pair, 0)
 
-    for copy in halos:
-        copy.wait_recv()
-
-    def halo_rows(step, carry):
-        rows = pl.ds(pl.multiple_of(step * ROWS, ROWS), ROWS)
-        b2 = halo_ref[0, :, 0, rows, :].astype(F32)
-        b1 = halo_ref[0, :, 1, rows, :].astype(F32)
-        a1 = halo_ref[1, :, 0, rows, :].astype(F32)
-        a2 = halo_ref[1, :, 1, rows, :].astype(F32)
-        last = plane_count - 1
-        for x, left, right in ((0, b2 - 8.0 * b1, b1), (last - 1, -a1, 8.0 * a1 - a2)):
+    last = plane_count - 1
+    share = 1.0 / 24.0
+
+    def turn_halo(side):
+        def halo_rows(step, carry):
+            rows = pl.ds(pl.multiple_of(step * ROWS, ROWS), ROWS)
+            first = halo_ref[side, :, 0, rows, :].astype(F32)
+            second = halo_ref[side, :, 1, rows, :].astype(F32)
+            if side == 0:
+                x, left, right = 0, first - 8.0 * second, second
+            else:
+                x, left, right = last - 1, -first, 8.0 * first - second
             moved = turn_pair(
                 swap_ref[...],
                 *[
@@ -355,9 +377,47 @@
                 field_ref[pl.ds((x + k) * width_y + step * ROWS, ROWS)] = moved[
                     :, k * LANES : (k + 1) * LANES
                 ].reshape(ROWS, band_pad, LANES)
-        return carry
-
-    lax.fori_loop(0, width_y // ROWS, halo_rows, 0)
+            return carry
+
+        lax.fori_loop(0, width_y // ROWS, halo_rows, 0)
+
+    def edge_side(side):
+        def edges(b, carry):
+            first = halo_ref[side, b, 0].astype(F32)
+            second = halo_ref[side, b, 1].astype(F32)
+            if side == 0:
+                x, left, right = 0, first - 16.0 * second, second
+            else:
+                x, left, right = last - 1, first, second - 16.0 * first
+            out_ref[b, x] = (edge_ref[b, 2 * side] + left * share).astype(BF16)
+            out_ref[b, x + 1] = (edge_ref[b, 2 * side + 1] + right * share).astype(BF16)
+            return carry
+
+        lax.fori_loop(0, band_count, edges, 0)
+        edge_copy(side).start()
+
+    even = lax.rem(own, 2) == 0
+
+    def on_sides(even_side, body):
+        @pl.when(even)
+        def _():
+            body(even_side)
+
+        @pl.when(jnp.logical_not(even))
+        def _():
+            body(1 - even_side)
+
+    def near_halo(side):
+        halos[side].wait_recv()
+        turn_halo(side)
+        edge_side(side)
+
+    def far_halo(side):
+        halos[side].wait_recv()
+        turn_halo(side)
+
+    on_sides(1, near_halo)
+    on_sides(0, far_halo)
 
     def fetch_halo(start, k, carry):
         tile = field_ref[pl.ds(rows_ref[start + k], depth)]
@@ -392,20 +452,7 @@
         copy.start()
         force_copies.append((slot, copy))
 
-    def edges(b, carry):
-        b2 = halo_ref[0, b, 0].astype(F32)
-        b1 = halo_ref[0, b, 1].astype(F32)
-        a1 = halo_ref[1, b, 0].astype(F32)
-        a2 = halo_ref[1, b, 1].astype(F32)
-        last = plane_count - 1
-        share = 1.0 / 24.0
-        out_ref[b, 0] = (edge_ref[b, 0] + (b2 - 16.0 * b1) * share).astype(BF16)
-        out_ref[b, 1] = (edge_ref[b, 1] + b1 * share).astype(BF16)
-        out_ref[b, last - 1] = (edge_ref[b, 2] + a1 * share).astype(BF16)
-        out_ref[b, last] = (edge_ref[b, 3] + (a2 - 16.0 * a1) * share).astype(BF16)
-        return carry
-
-    lax.fori_loop(0, band_count, edges, 0)
+    on_sides(0, edge_side)
     total = sums_ref[1]
     for slot, copy in force_copies:
         copy.wait_recv()
@@ -413,6 +460,14 @@
     force_ref[...] = total
     for copy in halos + copies + [copy for _, copy in force_copies]:
         copy.wait_send()
+
+    def finish(b, carry):
+        inner_copy(b).wait()
+        return carry
+
+    lax.fori_loop(0, band_count, finish, 0)
+    for side in range(2):
+        edge_copy(side).wait()
 
 
 def per_device(
@@ -439,12 +494,7 @@
     second_y = jnp.asarray(
         np.concatenate([second_y, np.eye(width_y, dtype=np.float32)], axis=1), BF16
     )
-    weights = jnp.pad(-2.0 * band_weights, (0, band_pad - band_count))[:, None]
     flat = projectors.reshape(entry_count * proj_count, tile_len)
-    row_line = jnp.pad(
-        tile_rows.astype(F32), (0, spots - entry_count), constant_values=-4096.0
-    )[None]
-
     moves = other_moves(dom_count)
     places = {u: 0 if u % dom_count == 0 else moves.index(u % dom_count) + 1 for u in range(-2, 3)}
     count = len(moves)
@@ -455,10 +505,11 @@
             jax.ShapeDtypeStruct(wavefunctions.shape, BF16),
             jax.ShapeDtypeStruct((8, LANES), F32),
         ),
-        in_specs=[pl.BlockSpec(memory_space=pl.ANY), vmem(), vmem(), vmem(), smem()]
-        + [vmem()] * 7,
-        out_specs=(vmem(), vmem()),
+        in_specs=[pl.BlockSpec(memory_space=pl.ANY), vmem(), vmem(), smem(), smem(), vmem(), smem()]
+        + [vmem()] * 4,
+        out_specs=(pl.BlockSpec(memory_space=pl.ANY), vmem()),
         scratch_shapes=[
+            pltpu.VMEM(wavefunctions.shape, BF16),
             pltpu.VMEM(wavefunctions.shape, BF16),
             pltpu.VMEM((2, band_count, 2, width_y, width_z), BF16),
             pltpu.VMEM(((plane_count + 4) * (width_y + 4), band_pad, width_z), BF16),
@@ -486,6 +537,7 @@
             pltpu.SemaphoreType.DMA((count,)),
             pltpu.SemaphoreType.DMA((slots,)),
             pltpu.SemaphoreType.DMA((slots,)),
+            pltpu.SemaphoreType.DMA((band_count + 2,)),
         ],
         compiler_params=pltpu.CompilerParams(
             vmem_limit_bytes=VMEM_LIMIT, collective_id=0, has_side_effects=True
@@ -495,8 +547,8 @@
         ),
         name="step",
     )(
-        wavefunctions, potential, flat, margin_atoms[:, None], tile_rows, row_line, coupling,
-        weights, swap, first_z, second_y, second_z,
+        wavefunctions, potential, flat, margin_atoms, tile_rows, coupling, band_weights, swap,
+        first_z, second_y, second_z,
     )
     return (applied, forces[:3, :ATOM_DEV])
 

time: 68.3 us -> 60.9 us (0.89)
  local copies, waits for them, and re-layouts: 12.9 us -> 6.04 us
  other arithmetic: 1.32 us -> 0 us
  Pallas kernels: 52.9 us -> 54 us
    unnamed x17 -> x1, local copies, waits for them, and re-layouts: 11.5 us -> 4.79 us
    pallas_call x1, Pallas kernels: 52.9 us -> 54 us  [per_device(): pl.pallas_call(functools.partial(whole_kernel, dims, dom_count, band_devi...]
    broadcast_in_dim x3 -> x0, local copies, waits for them, and re-layouts: 0.84 us -> none  [the longest x1 0.75 us: per_device(): margin_atoms[:, None]]
where the time goes in v3:
time: 60.9 us; the launch traced here: 60.7 us
  Pallas kernels  54 us (89%)
  local copies, waits for them, and re-layouts  6.04 us (10%)
  between operations  0.64 us (1%)
    pallas_call x1, Pallas kernels, per_device(): pl.pallas_call(functools.partial(whole_kernel, dims, dom_count, band_devi...  54 us
    unnamed x1, local copies, waits for them, and re-layouts  4.79 us
    slice x1, local copies, waits for them, and re-layouts, per_device(): return (applied, forces[:3, :ATOM_DEV])  1.25 us

profile of v3, /device:TPU:1, one launch (start us, length us, event | category | flops | bytes accessed | tf_op | source)
XLA Modules:
  0.0 60.7 jit_solution(13352598333750586119)
XLA Ops:
  0.6 54.0 %step.1 = (bf16[16,8,128,128]{3,2,1,0:T(8,128)(2,1)}, f32[8,128]{1,0:T(8,128)}) custom-call(bf16[16,8,128,128]{3,2,1,0:T(8,128)(2,1)} %wave_hbm.1, f32[8,128,128]{2,1,0:T(8,128)} %pot_ref.1, bf16[288,1024]{1,0:T(8,128)(2,1)} %bitcast.1, s32[36]{0:T(128)} %atoms_ref.1, s32[36]{0:T(128)} %rows_ref.1, f32[8,8]{1,0:T(8,128)} %coupling_ref.1, f32[16]{0:T(128)} %weight_ref.1, ...), custom_call_target="tpu_custom_call" | custom-call | flops 8589934592 | bytes 10485760 | tf_op jit(solution)/shard_map/step/pallas_call | solution.py:502
  54.6 1.3 %slice.3 = f32[3,12]{1,0:T(4,128)} slice(f32[8,128]{1,0:T(8,128)} %get-tuple-element.5), slice={[0:3], [0:12]} | slice | bytes 288 | tf_op jit(solution)/shard_map/slice | solution.py:553
  55.9 4.8 %copy.14 = bf16[16,8,128,128]{3,2,1,0:T(8,128)(2,1)} copy(bf16[16,8,128,128]{3,2,1,0:T(8,128)(2,1)} %get-tuple-element.8) | data formatting | bytes 8388608

commit v4 on v3

--- a/solution.py
+++ b/solution.py
@@ -52,10 +52,9 @@
 
 
 def pick_groups(whole, count, height, proj_count):
-    width = count * proj_count
-    whole = whole.reshape(count, height, width)
-    lane = lax.broadcasted_iota(jnp.int32, (count, height, width), 2) // proj_count
-    item = lax.broadcasted_iota(jnp.int32, (count, height, width), 0)
+    whole = whole.reshape(count, height, LANES)
+    lane = lax.broadcasted_iota(jnp.int32, whole.shape, 2) // proj_count
+    item = lax.broadcasted_iota(jnp.int32, whole.shape, 0)
     return jnp.sum(jnp.where(lane == item, whole, 0.0), axis=0)
 
 
@@ -89,7 +88,7 @@
 def whole_kernel(
     dims, dom_count, band_devices, places, wave_hbm, pot_ref, proj_ref, atoms_ref, rows_ref,
     coupling_ref, weight_ref, swap_ref, first_ref, second_y_ref, second_z_ref,
-    out_hbm, force_ref, out_ref, wave_ref, halo_ref, turned_ref, proj_z_ref, lhs_ref, margin_ref, meas_ref,
+    out_hbm, force_ref, out_ref, wave_ref, halo_ref, turned_ref, proj_pair_ref, lhs_ref, margin_ref, meas_ref,
     sort_ref, pick_ref, hit_ref, own_ref, table_ref, term_ref, part_ref, scale_ref, edge_ref,
     field_ref, extra_ref, sums_ref, held_ref, load_sem, halo_send, halo_recv, table_send,
     table_recv, force_send, force_recv, out_sem,
@@ -175,11 +174,18 @@
         grid_row = (iota((width_y, depth * spots), 0) + x * width_y).astype(F32)
         hit_ref[x * width_y : (x + 1) * width_y] = (grid_row == goal).astype(F32).astype(BF16)
     scale_ref[...] = (pot_ref[...] * -24.0).astype(BF16)
+    square = (LANES, LANES)
+    unit = (iota(square, 0) == iota(square, 1)).astype(F32).astype(BF16)
+    proj_pair_ref[...] = jnp.zeros_like(proj_pair_ref)
     for j in range(depth):
-        columns = slice(j * LANES, (j + 1) * LANES)
-        proj_z_ref[:, columns] = (
-            dot(proj_ref[:, columns], first_ref[...]) * (-1.0 / 12.0)
-        ).astype(BF16)
+        turned = dot_nt(unit, proj_ref[:, j * LANES : (j + 1) * LANES]).astype(BF16)
+        along_z = (dot(first_ref[...], turned) * (1.0 / 12.0)).astype(BF16)
+        for index, start in enumerate(range(0, entry_count, group)):
+            first = start * proj_count
+            width = min(group, entry_count - start) * proj_count
+            rows = slice(j * LANES, (j + 1) * LANES)
+            proj_pair_ref[index, rows, :width] = turned[:, first : first + width]
+            proj_pair_ref[index, rows, LANES : LANES + width] = along_z[:, first : first + width]
     meas_ref[...] = jnp.zeros_like(meas_ref)
     margin_ref[...] = jnp.zeros_like(margin_ref)
     extra_ref[...] = jnp.zeros_like(extra_ref)
@@ -187,16 +193,17 @@
 
     def turn(step, carry):
         rows = pl.ds(pl.multiple_of(step * ROWS, ROWS), ROWS)
-        for x in range(0, plane_count, 2):
-            moved = turn_pair(
-                swap_ref[...],
-                wave_ref[:, x, rows, :].reshape(band_count * ROWS, LANES),
-                wave_ref[:, x + 1, rows, :].reshape(band_count * ROWS, LANES),
-            )
-            for k in range(2):
-                turned_ref[pl.ds((x + k + 2) * stride + 2 + step * ROWS, ROWS)] = moved[
-                    :, k * LANES : (k + 1) * LANES
-                ].reshape(ROWS, band_pad, LANES)
+        blocks = [
+            wave_ref[:, x, rows, :].reshape(band_count * ROWS, LANES) for x in range(plane_count)
+        ]
+        moved = [
+            turn_pair(swap_ref[...], blocks[x], blocks[x + 1]) for x in range(0, plane_count, 2)
+        ]
+        for x in range(plane_count):
+            k = x % 2
+            turned_ref[pl.ds((x + 2) * stride + 2 + step * ROWS, ROWS)] = moved[x // 2][
+                :, k * LANES : (k + 1) * LANES
+            ].reshape(ROWS, band_pad, LANES)
         return carry
 
     lax.fori_loop(0, width_y // ROWS, turn, 0)
@@ -211,26 +218,30 @@
         at = row + j
         return at + 4 * lax.shift_right_logical(at, bits) + 2 * stride + 2
 
-    def each_group(body, height, weight_list):
-        for start in range(0, entry_count, group):
+    def each_group(body, height, results):
+        for index, start in enumerate(range(0, entry_count, group)):
             count = min(group, entry_count - start)
-            width = count * proj_count
             first = start * proj_count
-            lax.fori_loop(0, count, functools.partial(body, start), 0, unroll=4)
+
+            def step(pair, carry):
+                tiles = [body(rows_ref[start + 2 * pair + k]) for k in range(2)]
+                for k in range(2):
+                    lhs_ref[2 * pair + k, :height] = tiles[k]
+                return carry
+
+            lax.fori_loop(0, count // 2, step, 0, unroll=2)
             lhs = lhs_ref[:count, :height].reshape(count * height, depth * LANES)
-            for weight_ref_, result_ref, low in weight_list:
-                whole = dot_nt(lhs, weight_ref_[first : first + width])
-                result_ref[low : low + height, first : first + width] = pick_groups(
-                    whole, count, height, proj_count
+            width = len(results) * LANES
+            whole = dot(lhs, proj_pair_ref[index, :, :width])
+            for part, (result_ref, low) in enumerate(results):
+                result_ref[low : low + height, first : first + LANES] = pick_groups(
+                    whole[:, part * LANES : (part + 1) * LANES], count, height, proj_count
                 )
 
-    def fetch(start, k, carry):
-        row = rows_ref[start + k]
-        for j in range(depth):
-            lhs_ref[k, :band_pad, j * LANES : (j + 1) * LANES] = turned_ref[place(row, j)]
-        return carry
-
-    each_group(fetch, band_pad, [(proj_ref, margin_ref, 0), (proj_z_ref, meas_ref, 2 * band_pad)])
+    def fetch(row):
+        return jnp.concatenate([turned_ref[place(row, j)] for j in range(depth)], axis=1)
+
+    each_group(fetch, band_pad, [(margin_ref, 0), (meas_ref, 2 * band_pad)])
     own_ref[...] = dot(margin_ref[...].astype(BF16), sort_ref[...]).astype(BF16)
     copies = []
     for slot, u in enumerate(moves):
@@ -240,20 +251,19 @@
         copy.start()
         copies.append(copy)
 
-    def derive(start, k, carry):
-        row = rows_ref[start + k]
-        for j in range(depth):
-            at = place(row, j)
-            columns = slice(j * LANES, (j + 1) * LANES)
-            for part, step in ((0, stride), (1, 1)):
+    def derive(row):
+        parts = []
+        for step in (stride, 1):
+            values = []
+            for j in range(depth):
+                at = place(row, j)
                 far = turned_ref[at - 2 * step].astype(F32) - turned_ref[at + 2 * step].astype(F32)
                 side = turned_ref[at + step].astype(F32) - turned_ref[at - step].astype(F32)
-                lhs_ref[k, part * band_pad : (part + 1) * band_pad, columns] = (
-                    far * (1.0 / 12.0) + side * (2.0 / 3.0)
-                ).astype(BF16)
-        return carry
-
-    each_group(derive, 2 * band_pad, [(proj_ref, meas_ref, 0)])
+                values.append((far * (1.0 / 12.0) + side * (2.0 / 3.0)).astype(BF16))
+            parts.append(jnp.concatenate(values, axis=1))
+        return jnp.concatenate(parts, axis=0)
+
+    each_group(derive, 2 * band_pad, [(meas_ref, 0)])
 
     for copy in copies:
         copy.wait_recv()
@@ -313,35 +323,37 @@
     def each_pair(pair, carry):
         terms = jnp.concatenate([term_ref[pair * 2], term_ref[pair * 2 + 1]], axis=1)
         part_ref[...] = dot(hit_ref[...], terms).astype(BF16)
-        for x in range(plane_count):
-            tops, adds = [], []
-            for k in range(2):
-                b = pair * 2 + k
-
-                def near(offset):
-                    return [
-                        wave_ref[b, x + o]
-                        for o in (offset, -offset)
-                        if 0 <= x + o < plane_count
-                    ]
-
-                here = wave_ref[b, x]
-                one, two = near(1), near(2)
-                side = sum(one[1:], one[0]) * jnp.asarray(16.0, BF16)
-                side = side - sum(two[1:], two[0])
-                part = part_ref[x * width_y : (x + 1) * width_y, k * LANES : (k + 1) * LANES]
-                adds.append(side + (scale_ref[x] * here + part))
-                tops.append(here)
-            both = jnp.concatenate(
-                [jnp.concatenate(tops, axis=1), jnp.concatenate(adds, axis=1)], axis=0
-            )
-            lap = dot(second_y_ref[...], both)
-            along_z = dot(jnp.concatenate(tops, axis=0), second_z_ref[...])
-            for k in range(2):
-                b = pair * 2 + k
-                total = lap[:, k * LANES : (k + 1) * LANES]
-                total = total + along_z[k * width_y : (k + 1) * width_y]
-                total = total * (-1.0 / 24.0)
+        for start in range(0, plane_count, 2):
+            totals = []
+            for x in (start, start + 1):
+                tops, adds = [], []
+                for k in range(2):
+                    b = pair * 2 + k
+
+                    def near(offset):
+                        return [
+                            wave_ref[b, x + o]
+                            for o in (offset, -offset)
+                            if 0 <= x + o < plane_count
+                        ]
+
+                    here = wave_ref[b, x]
+                    one, two = near(1), near(2)
+                    side = sum(one[1:], one[0]) * jnp.asarray(16.0, BF16)
+                    side = side - sum(two[1:], two[0])
+                    part = part_ref[x * width_y : (x + 1) * width_y, k * LANES : (k + 1) * LANES]
+                    adds.append(side + (scale_ref[x] * here + part))
+                    tops.append(here)
+                both = jnp.concatenate(
+                    [jnp.concatenate(tops, axis=1), jnp.concatenate(adds, axis=1)], axis=0
+                )
+                lap = dot(second_y_ref[...], both)
+                along_z = dot(jnp.concatenate(tops, axis=0), second_z_ref[...])
+                for k in range(2):
+                    total = lap[:, k * LANES : (k + 1) * LANES]
+                    total = total + along_z[k * width_y : (k + 1) * width_y]
+                    totals.append((pair * 2 + k, x, total * (-1.0 / 24.0)))
+            for b, x, total in totals:
                 if x < 2:
                     edge_ref[b, x] = total
                 elif x >= plane_count - 2:
@@ -358,28 +370,34 @@
     share = 1.0 / 24.0
 
     def turn_halo(side):
-        def halo_rows(step, carry):
-            rows = pl.ds(pl.multiple_of(step * ROWS, ROWS), ROWS)
-            first = halo_ref[side, :, 0, rows, :].astype(F32)
-            second = halo_ref[side, :, 1, rows, :].astype(F32)
-            if side == 0:
-                x, left, right = 0, first - 8.0 * second, second
-            else:
-                x, left, right = last - 1, -first, 8.0 * first - second
-            moved = turn_pair(
-                swap_ref[...],
-                *[
-                    (value * (1.0 / 12.0)).astype(BF16).reshape(band_count * ROWS, LANES)
-                    for value in (left, right)
-                ],
-            )
+        def halo_rows(pair, carry):
+            moved = []
             for k in range(2):
-                field_ref[pl.ds((x + k) * width_y + step * ROWS, ROWS)] = moved[
-                    :, k * LANES : (k + 1) * LANES
-                ].reshape(ROWS, band_pad, LANES)
+                rows = pl.ds(pl.multiple_of((pair * 2 + k) * ROWS, ROWS), ROWS)
+                first = halo_ref[side, :, 0, rows, :].astype(F32)
+                second = halo_ref[side, :, 1, rows, :].astype(F32)
+                if side == 0:
+                    x, left, right = 0, first - 8.0 * second, second
+                else:
+                    x, left, right = last - 1, -first, 8.0 * first - second
+                moved.append(
+                    turn_pair(
+                        swap_ref[...],
+                        *[
+                            (value * (1.0 / 12.0)).astype(BF16).reshape(band_count * ROWS, LANES)
+                            for value in (left, right)
+                        ],
+                    )
+                )
+            for k in range(2):
+                for plane in range(2):
+                    at = (x + plane) * width_y + (pair * 2 + k) * ROWS
+                    field_ref[pl.ds(at, ROWS)] = moved[k][
+                        :, plane * LANES : (plane + 1) * LANES
+                    ].reshape(ROWS, band_pad, LANES)
             return carry
 
-        lax.fori_loop(0, width_y // ROWS, halo_rows, 0)
+        lax.fori_loop(0, width_y // ROWS // 2, halo_rows, 0)
 
     def edge_side(side):
         def edges(b, carry):
@@ -389,8 +407,10 @@
                 x, left, right = 0, first - 16.0 * second, second
             else:
                 x, left, right = last - 1, first, second - 16.0 * first
-            out_ref[b, x] = (edge_ref[b, 2 * side] + left * share).astype(BF16)
-            out_ref[b, x + 1] = (edge_ref[b, 2 * side + 1] + right * share).astype(BF16)
+            left = (edge_ref[b, 2 * side] + left * share).astype(BF16)
+            right = (edge_ref[b, 2 * side + 1] + right * share).astype(BF16)
+            out_ref[b, x] = left
+            out_ref[b, x + 1] = right
             return carry
 
         lax.fori_loop(0, band_count, edges, 0)
@@ -419,13 +439,10 @@
     on_sides(1, near_halo)
     on_sides(0, far_halo)
 
-    def fetch_halo(start, k, carry):
-        tile = field_ref[pl.ds(rows_ref[start + k], depth)]
-        for j in range(depth):
-            lhs_ref[k, :band_pad, j * LANES : (j + 1) * LANES] = tile[j]
-        return carry
-
-    each_group(fetch_halo, band_pad, [(proj_ref, extra_ref, 0)])
+    def fetch_halo(row):
+        return jnp.concatenate([field_ref[row + j] for j in range(depth)], axis=1)
+
+    each_group(fetch_halo, band_pad, [(extra_ref, 0)])
     sums = []
     for k in range(3):
         held = meas_ref[k * band_pad : (k + 1) * band_pad]
@@ -457,7 +474,7 @@
     for slot, copy in force_copies:
         copy.wait_recv()
         total = total + held_ref[slot]
-    force_ref[...] = total
+    force_ref[...] = total[:3, :ATOM_DEV]
     for copy in halos + copies + [copy for _, copy in force_copies]:
         copy.wait_send()
 
@@ -503,7 +520,7 @@
         functools.partial(whole_kernel, dims, dom_count, band_devices, places),
         out_shape=(
             jax.ShapeDtypeStruct(wavefunctions.shape, BF16),
-            jax.ShapeDtypeStruct((8, LANES), F32),
+            jax.ShapeDtypeStruct((3, ATOM_DEV), F32),
         ),
         in_specs=[pl.BlockSpec(memory_space=pl.ANY), vmem(), vmem(), smem(), smem(), vmem(), smem()]
         + [vmem()] * 4,
@@ -513,7 +530,7 @@
             pltpu.VMEM(wavefunctions.shape, BF16),
             pltpu.VMEM((2, band_count, 2, width_y, width_z), BF16),
             pltpu.VMEM(((plane_count + 4) * (width_y + 4), band_pad, width_z), BF16),
-            pltpu.VMEM((entry_count * proj_count, tile_len), BF16),
+            pltpu.VMEM((lanes // LANES, tile_len, 2 * LANES), BF16),
             pltpu.VMEM((group, 2 * band_pad, tile_len), BF16),
             pltpu.VMEM((band_pad, lanes), F32),
             pltpu.VMEM((3 * band_pad, lanes), F32),
@@ -550,7 +567,7 @@
         wavefunctions, potential, flat, margin_atoms, tile_rows, coupling, band_weights, swap,
         first_z, second_y, second_z,
     )
-    return (applied, forces[:3, :ATOM_DEV])
+    return (applied, forces)
 
 
 def other_moves(dom_count):

time: 60.9 us -> 59.1 us (0.970)
  Pallas kernels: 54 us -> 52.9 us
  local copies, waits for them, and re-layouts: 6.04 us -> 5.37 us
    slice x1 -> x0, local copies, waits for them, and re-layouts: 1.25 us -> none  [per_device(): return (applied, forces[:3, :ATOM_DEV])]
    pallas_call x1, Pallas kernels: 54 us -> 52.9 us  [per_device(): pl.pallas_call(functools.partial(whole_kernel, dims, dom_count, band_devi...]
    unnamed x1 -> x4, local copies, waits for them, and re-layouts: 4.79 us -> 5.37 us
where the time goes in v4:
time: 59.1 us; the launch traced here: 58.9 us
  Pallas kernels  52.9 us (90%)
  local copies, waits for them, and re-layouts  5.37 us (9%)
  between operations  0.65 us (1%)
    pallas_call x1, Pallas kernels, per_device(): pl.pallas_call(functools.partial(whole_kernel, dims, dom_count, band_devi...  52.9 us
    unnamed x4, local copies, waits for them, and re-layouts  5.37 us

profile of v4, /device:TPU:1, one launch (start us, length us, event | category | flops | bytes accessed | tf_op | source)
XLA Modules:
  0.0 58.9 jit_solution(4292277320748803980)
XLA Ops:
  0.6 52.9 %step.1 = (bf16[16,8,128,128]{3,2,1,0:T(8,128)(2,1)}, f32[3,12]{1,0:T(4,128)}) custom-call(bf16[16,8,128,128]{3,2,1,0:T(8,128)(2,1)} %wave_hbm.1, f32[8,128,128]{2,1,0:T(8,128)} %pot_ref.1, bf16[288,1024]{1,0:T(8,128)(2,1)} %bitcast.1, s32[36]{0:T(128)} %atoms_ref.1, s32[36]{0:T(128)} %rows_ref.1, f32[8,8]{1,0:T(8,128)} %coupling_ref.1, f32[16]{0:T(128)} %weight_ref.1, ...), custom_call_target="tpu_custom_call" | custom-call | flops 8589934592 | bytes 10485760 | tf_op jit(solution)/shard_map/step/pallas_call | solution.py:519
  53.5 0.0 copy-start
  53.5 4.8 %copy.15 = bf16[16,8,128,128]{3,2,1,0:T(8,128)(2,1)} copy(bf16[16,8,128,128]{3,2,1,0:T(8,128)(2,1)} %get-tuple-element.4) | data formatting | bytes 8388608
  58.3 0.0 copy-done
  58.3 0.6 copy.16
Async XLA Ops:
  53.5 4.8 %copy-start = (f32[3,12]{1,0:T(4,128)S(1)}, f32[3,12]{1,0:T(4,128)}, u32[]{:S(2)}) copy-start(f32[3,12]{1,0:T(4,128)} %get-tuple-element.5) | copy-start | bytes 436

commit v5 on v4

--- a/solution.py
+++ b/solution.py
@@ -11,6 +11,7 @@
 ATOM_DEV = 12
 LANES = 128
 ROWS = 16
+HALO_ROWS = 32
 VMEM_LIMIT = 62 * 1024 * 1024
 F32 = jnp.float32
 BF16 = jnp.bfloat16
@@ -121,18 +122,36 @@
     inner = (plane_count - 4) * width_y
     wait_all(greeted)
 
-    halos = [
-        remote(
-            wave_hbm.at[:, pl.ds(plane_count - 2, 2)], halo_ref.at[0], halo_send.at[0],
-            halo_recv.at[0], device(1, 0),
-        ),
-        remote(
-            wave_hbm.at[:, pl.ds(0, 2)], halo_ref.at[1], halo_send.at[1], halo_recv.at[1],
-            device(-1, 0),
-        ),
-    ]
-    for copy in halos:
-        copy.start()
+    pieces = width_y // HALO_ROWS
+    halos = []
+    for side in range(2):
+        planes = pl.ds((plane_count - 2) * (1 - side), 2)
+        for piece in range(pieces):
+            rows = pl.ds(piece * HALO_ROWS, HALO_ROWS)
+            slot = side * pieces + piece
+            halos.append(
+                remote(
+                    wave_hbm.at[:, planes, rows], halo_ref.at[side, :, :, rows],
+                    halo_send.at[slot], halo_recv.at[slot], device(1 - 2 * side, 0),
+                )
+            )
+    even = lax.rem(own, 2) == 0
+
+    def on_sides(even_side, body):
+        @pl.when(even)
+        def _():
+            body(even_side)
+
+        @pl.when(jnp.logical_not(even))
+        def _():
+            body(1 - even_side)
+
+    def start_halo(side):
+        for piece in range(pieces):
+            halos[side * pieces + piece].start()
+
+    on_sides(1, start_halo)
+    on_sides(0, start_halo)
 
     field_ref[2 * width_y : 2 * width_y + inner] = jnp.zeros((inner, band_pad, LANES), BF16)
     spots = lanes // proj_count
@@ -370,7 +389,7 @@
     share = 1.0 / 24.0
 
     def turn_halo(side):
-        def halo_rows(pair, carry):
+        def halo_rows(pair):
             moved = []
             for k in range(2):
                 rows = pl.ds(pl.multiple_of((pair * 2 + k) * ROWS, ROWS), ROWS)
@@ -395,9 +414,10 @@
                     field_ref[pl.ds(at, ROWS)] = moved[k][
                         :, plane * LANES : (plane + 1) * LANES
                     ].reshape(ROWS, band_pad, LANES)
-            return carry
-
-        lax.fori_loop(0, width_y // ROWS // 2, halo_rows, 0)
+
+        for piece in range(pieces):
+            halos[side * pieces + piece].wait_recv()
+            halo_rows(piece)
 
     def edge_side(side):
         def edges(b, carry):
@@ -416,28 +436,12 @@
         lax.fori_loop(0, band_count, edges, 0)
         edge_copy(side).start()
 
-    even = lax.rem(own, 2) == 0
-
-    def on_sides(even_side, body):
-        @pl.when(even)
-        def _():
-            body(even_side)
-
-        @pl.when(jnp.logical_not(even))
-        def _():
-            body(1 - even_side)
-
     def near_halo(side):
-        halos[side].wait_recv()
         turn_halo(side)
         edge_side(side)
 
-    def far_halo(side):
-        halos[side].wait_recv()
-        turn_halo(side)
-
     on_sides(1, near_halo)
-    on_sides(0, far_halo)
+    on_sides(0, turn_halo)
 
     def fetch_halo(row):
         return jnp.concatenate([field_ref[row + j] for j in range(depth)], axis=1)
@@ -548,8 +552,8 @@
             pltpu.VMEM((3, 8, LANES), F32),
             pltpu.VMEM((slots, 8, LANES), F32),
             pltpu.SemaphoreType.DMA,
-            pltpu.SemaphoreType.DMA((2,)),
-            pltpu.SemaphoreType.DMA((2,)),
+            pltpu.SemaphoreType.DMA((2 * width_y // HALO_ROWS,)),
+            pltpu.SemaphoreType.DMA((2 * width_y // HALO_ROWS,)),
             pltpu.SemaphoreType.DMA((count,)),
             pltpu.SemaphoreType.DMA((count,)),
             pltpu.SemaphoreType.DMA((slots,)),

time: 59.1 us -> 59.2 us (level)
  no operation moved by 1% of the time
where the time goes in v5:
time: 59.2 us; the launch traced here: 59 us
  Pallas kernels  53 us (90%)
  local copies, waits for them, and re-layouts  5.37 us (9%)
  between operations  0.65 us (1%)
    pallas_call x1, Pallas kernels, per_device(): pl.pallas_call(functools.partial(whole_kernel, dims, dom_count, band_devi...  53 us
    unnamed x4, local copies, waits for them, and re-layouts  5.37 us

profile of v5, /device:TPU:1, one launch (start us, length us, event | category | flops | bytes accessed | tf_op | source)
XLA Modules:
  0.0 59.0 jit_solution(8540934118654926493)
XLA Ops:
  0.6 53.0 %step.1 = (bf16[16,8,128,128]{3,2,1,0:T(8,128)(2,1)}, f32[3,12]{1,0:T(4,128)}) custom-call(bf16[16,8,128,128]{3,2,1,0:T(8,128)(2,1)} %wave_hbm.1, f32[8,128,128]{2,1,0:T(8,128)} %pot_ref.1, bf16[288,1024]{1,0:T(8,128)(2,1)} %bitcast.1, s32[36]{0:T(128)} %atoms_ref.1, s32[36]{0:T(128)} %rows_ref.1, f32[8,8]{1,0:T(8,128)} %coupling_ref.1, f32[16]{0:T(128)} %weight_ref.1, ...), custom_call_target="tpu_custom_call" | custom-call | flops 8589934592 | bytes 10485760 | tf_op jit(solution)/shard_map/step/pallas_call | solution.py:523
  53.6 0.0 copy-start
  53.6 4.8 %copy.15 = bf16[16,8,128,128]{3,2,1,0:T(8,128)(2,1)} copy(bf16[16,8,128,128]{3,2,1,0:T(8,128)(2,1)} %get-tuple-element.4) | data formatting | bytes 8388608
  58.4 0.0 copy-done
  58.4 0.6 copy.16
Async XLA Ops:
  53.6 4.8 %copy-start = (f32[3,12]{1,0:T(4,128)S(1)}, f32[3,12]{1,0:T(4,128)}, u32[]{:S(2)}) copy-start(f32[3,12]{1,0:T(4,128)} %get-tuple-element.5) | copy-start | bytes 436
